TPU v7x, 256 devices: a whole 4x4x8 slice. The times are simulated.
256 devices in a mesh: pb: 8 (over y, x_lo), ha: 8 (over z), ka: 4 (over x_hi, core).
Axes of the slice: x: 4 (x_hi: 2, x_lo: 2; x = x_hi * 2 + x_lo), y: 4, z: 8, core: 2. Of those that a mesh axis runs over, the one named last changes fastest.
Arguments:
- main_query: bfloat16 [2048, 128, 192], P('pb', 'ha'), may hold values from -210 to 210
- main_key: bfloat16 [8192, 128, 192], P('ka', 'ha'), may hold values from -6 to 6
- index_query: bfloat16 [2048, 64, 128], P('pb', 'ha'), may hold values from -45 to 45
- index_weight: bfloat16 [2048, 64], P('pb', 'ha'), may hold values from -0.099609375 to 0.29882812
- index_key: bfloat16 [8192, 128], P(('pb', 'ka')), may hold values from -6 to 6
- query_pos: int32 [2048], P('pb'), may hold values from 1 to 8191
Outputs:
- grad_query: float32 [2048, 64, 128], P(('pb', 'ka'), 'ha')
- grad_weight: float32 [2048, 64], P(('pb', 'ka'), 'ha')
- grad_key: float32 [8192, 128], P(('pb', 'ka'))
All inputs are finite; a program needn't handle non-finite values.
Results may differ from a plain program's by a relative error of at most 0.00095.
Values may be sent and summed in bfloat16 or wider, within the bound.
A program may use at most 192 MiB of HBM per device.

v0:
```python
import math

import jax
import jax.numpy as jnp
from jax import lax
from jax.sharding import PartitionSpec as P

floor_value = -1e30


def combined_all(value, axis, join):
    pieces = jax.tree.map(lambda part: lax.all_gather(part, axis), value)
    head = jax.tree.map(lambda part: part[0], pieces)
    tail = jax.tree.map(lambda part: part[1:], pieces)
    subtotal, _ = lax.scan(lambda subtotal, slab: (join(subtotal, slab), None), head, tail)
    return subtotal


def joined(first, second):
    top = jnp.maximum(first[0], second[0])
    return (top, first[1] * jnp.exp(first[0] - top) + second[1] * jnp.exp(second[0] - top))


def local_stats(values, visible):
    masked = jnp.where(visible, values, floor_value)
    maxima = jnp.max(masked, axis=-1)
    expos = jnp.where(visible, jnp.exp(masked - maxima[..., None]), 0.0)
    return (maxima, expos, jnp.sum(expos, axis=-1))


def body(main_query, main_key, index_query, index_weight, index_key, query_pos):
    key_count = main_key.shape[0]
    main_heads = main_query.shape[1]
    head_size = main_query.shape[2]
    index_size = index_query.shape[2]
    key_total = key_count * lax.axis_size("ka")
    scale = 1.0 / math.sqrt(index_size)
    ctx_key = lax.all_gather(index_key, "pb", axis=0, tiled=True)
    key_ids = lax.axis_index("ka") * key_count + jnp.arange(key_count, dtype=jnp.int32)
    visible = key_ids[None, :] <= query_pos[:, None]
    scores = jnp.einsum(
        "thd,shd->hts", main_query, main_key, preferred_element_type=jnp.float32
    ) / math.sqrt(head_size)
    maxima, expos, totals = local_stats(scores, visible[None])
    glob_max, glob_total = combined_all((maxima, totals), "ka", joined)
    factor = jnp.exp(maxima - glob_max) / glob_total / (main_heads * lax.axis_size("ha"))
    target_part = jnp.einsum("hts,ht->ts", expos, factor)
    acts = (
        jnp.einsum("tjd,sd->jts", index_query, ctx_key, preferred_element_type=jnp.float32) * scale
    )
    weights_wide = index_weight.astype(jnp.float32).T
    logit_part = jnp.sum(weights_wide[:, :, None] * jnp.maximum(acts, 0.0), axis=0)
    target, logits = lax.psum((target_part, logit_part), "ha")
    row_max, row_expos, row_total = local_stats(logits, visible)
    glob_max, glob_total = combined_all((row_max, row_total), "ka", joined)
    prob = row_expos * (jnp.exp(row_max - glob_max) / glob_total)[:, None]
    diff = (prob - target) * (key_total / 16.0)
    relu_act = jnp.maximum(acts, 0.0)
    weight_part = jnp.sum(diff[None] * relu_act, axis=2).T
    gate = jnp.where(acts > 0, diff[None] * weights_wide[:, :, None], 0.0)
    query_part = (
        jnp.einsum(
            "jts,sd->tjd", gate, ctx_key.astype(jnp.float32), precision=lax.Precision.HIGHEST
        )
        * scale
    )
    key_part = (
        jnp.einsum(
            "jts,tjd->sd", gate, index_query.astype(jnp.float32), precision=lax.Precision.HIGHEST
        )
        * scale
    )
    grad_query, grad_weight = (
        lax.psum_scatter(query_part, "ka", scatter_dimension=0, tiled=True),
        lax.psum_scatter(weight_part, "ka", scatter_dimension=0, tiled=True),
    )
    block_sum = lax.psum_scatter(key_part, "pb", scatter_dimension=0, tiled=True)
    grad_key = lax.psum(block_sum, "ha")
    return (grad_query, grad_weight, grad_key)


def solution(mesh):
    placed = (
        P("pb", "ha", None),
        P("ka", "ha", None),
        P("pb", "ha", None),
        P("pb", "ha"),
        P(("pb", "ka"), None),
        P("pb"),
    )
    return jax.shard_map(
        body,
        mesh=mesh,
        in_specs=placed,
        out_specs=(P(("pb", "ka"), "ha", None), P(("pb", "ka"), "ha"), P(("pb", "ka"), None)),
        check_vma=False,
    )
```

profile of v0, /device:TPU:8, one launch (start us, length us, event | category | flops | bytes accessed | tf_op | source)
XLA Modules:
  0.0 475.3 jit_solution(15598652891153235353)
XLA Ops:
  7.2 1.2 broadcast_compare_fusion
  8.5 1.0 copy.15
  9.6 19.6 %fusion.2 = (f32[16,256]{1,0:T(8,128)S(1)}, f32[16,256,2048]{2,1,0:T(8,128)}) fusion(pred[256,2048]{1,0:T(8,128)(4,1)S(1)} %copy.15, bf16[256,16,192]{0,2,1:T(8,128)(2,1)S(1)} %copy-done, bf16[2048,16,192]{0,2,1:T(8,128)(2,1)} %param.11), kind=kOutput, calls=%fused_computation.11 | convolution fusion | flops 3246387200 | bytes 48250880 | tf_op jit(solution)/shard_map/thd,shd->hts/dot_general | solution.py:41
  29.1 15.6 %fusion.3 = f32[16,256]{1,0:T(8,128)S(1)} fusion(f32[16,256,2048]{2,1,0:T(8,128)} %get-tuple-element.100, f32[16,256]{1,0:T(8,128)S(1)} %get-tuple-element.99, pred[256,2048]{1,0:T(8,128)(4,1)S(1)} %copy.15), kind=kLoop, calls=%fused_computation.12 | loop fusion | flops 41938944 | bytes 34111488 | tf_op jit(solution)/shard_map/reduce_sum | solution.py:28
  44.7 6.8 %all-gather.3 = f32[64,256]{1,0:T(8,128)S(1)} all-gather(f32[16,256]{1,0:T(8,128)S(1)} %fusion.3), channel_id=5, replica_groups=mesh['pb'=8,'ha'=8,'ka'=4] {'ka'}, dimensions={0}, use_global_device_ids=true | all-gather | bytes 81920 | tf_op jit(solution)/shard_map/all_gather | solution.py:12
  51.5 6.7 %all-gather.2 = f32[64,256]{1,0:T(8,128)S(1)} all-gather(f32[16,256]{1,0:T(8,128)S(1)} %get-tuple-element.99), channel_id=4, replica_groups=mesh['pb'=8,'ha'=8,'ka'=4] {'ka'}, dimensions={0}, use_global_device_ids=true | all-gather | bytes 81920 | tf_op jit(solution)/shard_map/all_gather | solution.py:12
  58.2 0.1 while.25
  58.4 17.2 %multiply_reduce_fusion = f32[256,2048]{1,0:T(8,128)} fusion(f32[16,256,2048]{2,1,0:T(8,128)} %get-tuple-element.100, f32[256,16]{0,1:T(8,128)S(1)} %multiply_bitcast_fusion, f32[16,256]{1,0:T(8,128)S(1)} %get-tuple-element.99, pred[256,2048]{1,0:T(8,128)(4,1)S(1)} %copy.15), kind=kLoop, calls=%fused_computation.8 | loop fusion | flops 49807360 | bytes 36208640
  75.6 2.9 copy.25
  78.5 29.7 %all_gather.27 = bf16[2048,128]{1,0:T(8,128)(2,1)S(1)} all-gather(bf16[256,128]{1,0:T(8,128)(2,1)S(1)} %copy-done.3), channel_id=1, replica_groups=mesh['pb'=8,'ha'=8,'ka'=4] {'pb'}, dimensions={0}, use_global_device_ids=true | all-gather | bytes 589824 | tf_op jit(solution)/shard_map/all_gather | solution.py:38
  108.2 8.7 %multiply_compare_fusion = (pred[2048,256,8]{1,0,2:T(32,128)(4,1)}, f32[2048,256,8]{1,0,2:T(8,128)}) fusion(bf16[256,8,128]{2,1,0:T(8,128)(2,1)S(1)} %copy-done.6, bf16[2048,128]{1,0:T(8,128)(2,1)S(1)} %all_gather.27), kind=kOutput, calls=%fused_computation.22 | convolution fusion | flops 1082130432 | bytes 22020096 | tf_op jit(solution)/shard_map/tjd,sd->jts/dot_general | solution.py:49
  117.0 9.6 %fusion.4 = f32[256,2048]{0,1:T(8,128)} fusion(f32[2048,256,8]{1,0,2:T(8,128)} %get-tuple-element.98, f32[8,256]{1,0:T(8,128)S(1)} %convert_bitcast_fusion), kind=kLoop, calls=%fused_computation.15 | loop fusion | flops 16252928 | bytes 18882560 | tf_op jit(solution)/shard_map/reduce_sum | solution.py:52
  126.6 112.5 %all-reduce.6.cloned.1.call-done = (f32[256,2048]{0,1:T(8,128)}, f32[256,2048]{0,1:T(8,128)}) async-done(((f32[256,2048]{0,1:T(8,128)}, f32[256,2048]{0,1:T(8,128)}), (f32[256,2048]{0,1:T(8,128)}, f32[256,2048]{0,1:T(8,128)})) %all-reduce.6.cloned.1.call-update) | async-done | bytes 4194320 | tf_op jit(solution)/shard_map/psum | solution.py:53
  239.1 1.8 fusion.19
  240.8 1.9 fusion.18
  242.7 6.6 %all-gather.5 = f32[4,1,256]{2,1,0:T(1,128)S(1)} all-gather(f32[1,1,256]{2,1,0:T(1,128)S(1)} %bitcast.89), channel_id=3, replica_groups=mesh['pb'=8,'ha'=8,'ka'=4] {'ka'}, dimensions={0}, use_global_device_ids=true | all-gather | bytes 5120 | tf_op jit(solution)/shard_map/all_gather | solution.py:12
  249.3 6.6 %all-gather.4 = f32[4,1,256]{2,1,0:T(1,128)S(1)} all-gather(f32[1,1,256]{2,1,0:T(1,128)S(1)} %bitcast.86), channel_id=2, replica_groups=mesh['pb'=8,'ha'=8,'ka'=4] {'ka'}, dimensions={0}, use_global_device_ids=true | all-gather | bytes 5120 | tf_op jit(solution)/shard_map/all_gather | solution.py:12
  255.9 0.1 while.24
  256.1 2.6 subtract_multiply_fusion
  258.7 1.3 copy-done.2
  260.0 18.2 %fusion.17 = f32[2048,128]{1,0:T(8,128)} fusion(pred[2048,256,8]{1,0,2:T(32,128)(4,1)} %get-tuple-element.97, f32[256,2048]{0,1:T(8,128)S(1)} %subtract_multiply_fusion, f32[8,256]{1,0:T(8,128)S(1)} %convert_bitcast_fusion, bf16[256,8,128]{2,1,0:T(8,128)(2,1)S(1)} %copy-done.6), kind=kOutput, calls=%fused_computation.30 | convolution fusion | flops 6451101696 | bytes 7872512 | tf_op jit(solution)/shard_map/jts,tjd->sd/dot_general | solution.py:68
  278.2 8.5 %fusion.5 = f32[8,256]{1,0:T(8,128)S(1)} fusion(f32[2048,256,8]{1,0,2:T(8,128)} %get-tuple-element.98, f32[256,2048]{0,1:T(8,128)} %copy-done.2), kind=kLoop, calls=%fused_computation.16 | loop fusion | flops 16775168 | bytes 18882560 | tf_op jit(solution)/shard_map/reduce_sum | solution.py:59
  286.8 0.8 copy.27
  287.6 0.3 reduce-scatter.6.cloned.1.call-start
  287.9 16.8 %fusion.21 = f32[256,8,128]{2,0,1:T(8,128)} fusion(pred[2048,256,8]{1,0,2:T(32,128)(4,1)} %get-tuple-element.97, f32[256,2048]{0,1:T(8,128)} %copy-done.2, f32[8,256]{1,0:T(8,128)S(1)} %convert_bitcast_fusion, bf16[2048,128]{1,0:T(8,128)(2,1)S(1)} %all_gather.27), kind=kOutput, calls=%fused_computation.37 | convolution fusion | flops 6451101696 | bytes 7872512 | tf_op jit(solution)/shard_map/jts,sd->tjd/dot_general | solution.py:62
  304.7 13.8 %reduce-scatter.8.cloned.1.call-done = f32[256,128]{1,0:T(8,128)} async-done(((f32[2048,128]{1,0:T(8,128)}), f32[256,128]{1,0:T(8,128)}) %reduce-scatter.8.cloned.1.call-update) | async-done | bytes 131088 | tf_op jit(solution)/shard_map/reduce_scatter | solution.py:77
  318.5 35.9 %reduce-scatter.10.cloned.1.call-done = f32[64,8]{1,0:T(8,128)} async-done(((f32[256,8]{1,0:T(8,128)}), f32[64,8]{1,0:T(8,128)}) %reduce-scatter.10.cloned.1.call-update) | async-done | bytes 2064
  354.4 1.4 copy.28
  355.8 37.9 %reduce-scatter.6.cloned.1.call-done = f32[64,8,128]{2,0,1:T(8,128)} async-done(((f32[256,8,128]{2,0,1:T(8,128)}), f32[64,8,128]{2,0,1:T(8,128)}) %reduce-scatter.6.cloned.1.call-update) | async-done | bytes 262160 | tf_op jit(solution)/shard_map/reduce_scatter | solution.py:74
  393.7 1.8 copy.18
  395.5 71.8 %all-reduce.4.cloned.1.call-done = f32[256,128]{1,0:T(8,128)} async-done(((f32[256,128]{1,0:T(8,128)}), f32[256,128]{1,0:T(8,128)}) %all-reduce.4.cloned.1.call-update) | async-done | bytes 131088 | tf_op jit(solution)/shard_map/psum | solution.py:78
  467.2 1.6 copy.67
  (45 shorter events, 0.5 us)
Async XLA Ops:
  7.2 2.4 copy-start
  7.2 231.9 %all-reduce.6.cloned.1.call-start = ((), (), s32[]{:S(2)}) async-start(), calls=%async_computation.7 | async-start | bytes 8388608 | tf_op jit(solution)/shard_map/psum | solution.py:53
  58.4 20.2 %copy-start.3 = (bf16[256,128]{1,0:T(8,128)(2,1)S(1)}, bf16[256,128]{1,0:T(8,128)(2,1)}, u32[]{:S(2)}) copy-start(bf16[256,128]{1,0:T(8,128)(2,1)} %param.14) | copy-start | bytes 196612
  58.4 49.8 %copy-start.5 = (bf16[256,8]{0,1:T(8,128)(2,1)S(1)}, bf16[256,8]{0,1:T(8,128)(2,1)}, u32[]{:S(2)}) copy-start(bf16[256,8]{0,1:T(8,128)(2,1)} %param.13) | copy-start | bytes 12292
  58.4 49.8 %copy-start.6 = (bf16[256,8,128]{2,1,0:T(8,128)(2,1)S(1)}, bf16[256,8,128]{2,1,0:T(8,128)(2,1)}, u32[]{:S(2)}) copy-start(bf16[256,8,128]{2,1,0:T(8,128)(2,1)} %param.12) | copy-start | bytes 1572868
  117.0 122.1 %copy-start.4 = (s32[256]{0:T(256)S(1)}, s32[256]{0:T(256)}, u32[]{:S(2)}) copy-start(s32[256]{0:T(256)} %param.15) | copy-start | bytes 3076
  126.5 192.0 %reduce-scatter.8.cloned.1.call-start = ((), (), s32[]{:S(2)}) async-start(), calls=%async_computation.4 | async-start | bytes 1179648 | tf_op jit(solution)/shard_map/reduce_scatter | solution.py:77
  258.6 1.3 copy-start.2
  278.2 76.2 %reduce-scatter.10.cloned.1.call-start = ((), (), s32[]{:S(2)}) async-start(), calls=%async_computation.6 | async-start | bytes 163840
  287.6 181.2 %copy-start.1 = (bf16[256,16,192]{0,2,1:T(8,128)(2,1)S(1)}, bf16[256,16,192]{0,2,1:T(8,128)(2,1)}, u32[]{:S(2)}) copy-start(bf16[256,16,192]{0,2,1:T(8,128)(2,1)} %param.10) | copy-start | bytes 4718596
  287.6 106.0 %reduce-scatter.6.cloned.1.call-start = ((), (), s32[]{:S(2)}) async-start(), calls=%async_computation.3 | async-start | bytes 1310720 | tf_op jit(solution)/shard_map/reduce_scatter | solution.py:74
  304.7 162.5 %all-reduce.4.cloned.1.call-start = ((), (), s32[]{:S(2)}) async-start(), calls=%async_computation.5 | async-start | bytes 262144 | tf_op jit(solution)/shard_map/psum | solution.py:78
Sparse Core Ops, SparseCore 0:
  126.6 112.3 all-reduce.5
  278.3 40.1 reduce-scatter.7
  321.8 32.5 reduce-scatter.9
  357.2 36.3 reduce-scatter.5
  395.8 71.3 all-reduce.3
where the time goes:
time: 476 us; the launch traced here: 475 us
  waiting for transfers between devices  272 us (57%)
  matrix products  63.3 us (13%)
  other arithmetic  58.5 us (12%)
  blocking collectives  56.3 us (12%)
  between operations  13.9 us (3%)
  local copies, waits for them, and re-layouts  11 us (2%)
    psum x1, waiting for transfers between devices, body(): target, logits = lax.psum((target_part, logit_part), 'ha')  112 us
    psum x1, waiting for transfers between devices, body(): grad_key = lax.psum(block_sum, 'ha')  71.8 us
    reduce_scatter x1, waiting for transfers between devices, body(): lax.psum_scatter(query_part, 'ka', scatter_dimension=0, tiled=True)  37.9 us
    unnamed x6, waiting for transfers between devices  35.9 us
    all_gather x1, blocking collectives, body(): ctx_key = lax.all_gather(index_key, 'pb', axis=0, tiled=True)  29.7 us
    all_gather x4, blocking collectives, combined_all(): pieces = jax.tree.map(lambda part: lax.all_gather(part, axis), value)  26.6 us
    dot_general x1, matrix products, body(): jnp.einsum('thd,shd->hts', main_query, main_key, preferred_element_type=j...  19.6 us
    dot_general x1, matrix products, body(): jnp.einsum('jts,tjd->sd', gate, index_query.astype(jnp.float32), precisio...  18.2 us
  transfers between devices with their start and end apart: 5, of which 5 were waited for; matrix products, arithmetic and copies ran while one was open for 6% of the time, Pallas kernels for 0%

commit v1 on v0

v1 whole, which is shorter than its diff:
```python
import functools
import math

import jax
import jax.numpy as jnp
from jax import lax
from jax.experimental import pallas as pl
from jax.experimental.pallas import tpu as pltpu
from jax.sharding import PartitionSpec as P

MESH = pl.DeviceIdType.MESH
LOW = -1e30
LANES = 128
NBUF = 4
EXTRA = 6
LOG2E = 1.4426950408889634


def lane_spread(row):
    return jnp.transpose(jnp.broadcast_to(row, (LANES, LANES)), (1, 0))


def kernel(
    dims,
    q_ref, kt_ref, pos_ref, iq_ref, wc_ref, wn_ref, ik_ref,
    gq_ref, gw_ref, gk_ref,
    kbuf, s0, s1, e_ref, f_ref, stm, stl, st_tx, st_rx, comb,
    t_ref, rxa, rxb,
    iq_all, wc_all, w_rep, wq_t, ctx, ctx_t, m_ref, lg, d_hi, d_lo,
    ix_tx, ix_rx,
    u_ref, u_rx, v_ref, v_rx, r_ref, o_rx,
    gk_tx, gk_rx, z_tx, z_rx, zsum,
    ksem, st_s, st_r, ra_s, ra_r, rb_s, rb_r, iq_s, iq_r, wc_s, wc_r, cx_s, cx_r,
    ix_s, ix_r, u_s, u_r, v_s, v_r, o_s, o_r, gk_s, gk_r, z_s, z_r, y_s, y_r,
):
    n_pb, n_ha, n_ka, heads, dh, keys, main_total, key_total = dims
    p, h, k = lax.axis_index("pb"), lax.axis_index("ha"), lax.axis_index("ka")
    half = n_ha // 2
    rows = half * 32
    groups = rows // 8
    tiles = keys // LANES
    slots = heads + EXTRA
    scale_main = LOG2E / math.sqrt(dh)
    scale = 1.0 / math.sqrt(128)

    offsets = [half]
    for o in range(half - 1, 0, -1):
        offsets += [-o, o]
    offsets += [0]

    def copy_to(src, dst, ss, rs, dev):
        return pltpu.make_async_remote_copy(
            src_ref=src, dst_ref=dst, send_sem=ss, recv_sem=rs, device_id=dev, device_id_type=MESH
        )

    def pb_dev(i):
        return {"pb": lax.rem(p + i, n_pb)}

    def ha_dev(i):
        return {"ha": lax.rem(h + i + n_ha, n_ha)}

    def ka_dev(i):
        return {"ka": lax.rem(k + i, n_ka)}

    def kcopy(head, slot):
        return pltpu.make_async_copy(kt_ref.at[head], kbuf.at[slot], ksem.at[slot])

    for n in range(NBUF):
        kcopy(n, n).start()

    barrier = pltpu.get_barrier_semaphore()
    for i in range(1, n_ha):
        pl.semaphore_signal(barrier, inc=1, device_id=ha_dev(i), device_id_type=MESH)
    for i in range(1, n_pb):
        pl.semaphore_signal(barrier, inc=1, device_id=pb_dev(i), device_id_type=MESH)
    for i in range(1, n_ka):
        pl.semaphore_signal(barrier, inc=1, device_id=ka_dev(i), device_id_type=MESH)
    pl.semaphore_wait(barrier, n_ha + n_pb + n_ka - 3)

    def iq_copy(i):
        dest = lax.rem(h + i, n_ha)
        return copy_to(
            iq_ref.at[:, pl.ds(pl.multiple_of(dest * 64, 64), 64), :],
            iq_all.at[:, pl.ds(pl.multiple_of(h * 64, 64), 64), :],
            iq_s.at[i], iq_r.at[i], ha_dev(i),
        )

    def wc_copy(i):
        dest = lax.rem(h + i, n_ha)
        return copy_to(wc_ref.at[dest], wc_all.at[h], wc_s.at[i], wc_r.at[i], ha_dev(i))

    def cx_copy(i):
        return copy_to(
            ik_ref, ctx.at[pl.ds(pl.multiple_of(p * 256, 256), 256), :], cx_s.at[i], cx_r.at[i], pb_dev(i)
        )

    for i in range(1, n_pb):
        cx_copy(i).start()
    for i in range(1, n_ha):
        iq_copy(i).start()
        wc_copy(i).start()

    lane = lax.broadcasted_iota(jnp.int32, (8, LANES), 1)
    lane_rows = lax.broadcasted_iota(jnp.int32, (rows, LANES), 1)
    first_key = k * keys

    def dest_of(i):
        return lax.rem(h + offsets[i] + n_ha, n_ha)

    def scores(st, head, slot, out):
        q = jnp.concatenate([q_ref[head, dest_of(st * half + i)] for i in range(half)], axis=0)
        out[...] = jnp.dot(q, kbuf[slot], preferred_element_type=jnp.float32)

    def eslot(st, head):
        return lax.rem(st * heads + head, slots) if not isinstance(head, int) else (st * heads + head) % slots

    def soften(st, head, src):
        slot = eslot(st, head)
        tops, sums = [], []
        for g in range(groups):
            rel = pos_ref[dest_of(st * half + g // 4), pl.ds((g % 4) * 8, 8), :] - first_key - lane
            x = [
                jnp.where(rel >= c * LANES, src[g * 8 : g * 8 + 8, c * LANES : (c + 1) * LANES], LOW)
                for c in range(tiles)
            ]
            top = functools.reduce(jnp.maximum, x)
            total = None
            for c in range(tiles):
                e = jnp.exp2((x[c] - top) * scale_main)
                e_ref[slot, g * 8 : g * 8 + 8, c * LANES : (c + 1) * LANES] = e
                total = e if total is None else total + e
            tops.append(top)
            sums.append(total)
        tops = jnp.concatenate(tops, axis=0)
        sums = jnp.concatenate(sums, axis=0)
        f_ref[st, head] = tops
        row_top = jnp.max(tops, axis=1, keepdims=True)
        row_sum = jnp.sum(sums * jnp.exp2((tops - row_top) * scale_main), axis=1, keepdims=True)
        stm[...] = jnp.where(lane_rows == head, row_top, stm[...])
        stl[...] = jnp.where(lane_rows == head, row_sum, stl[...])

    def st_copy(st, i):
        return copy_to(st_tx.at[st], st_rx.at[st, i], st_s.at[st, i], st_r.at[st, i], ka_dev(i))

    def send_stats(st):
        st_tx[st, 0:heads] = jnp.transpose(stm[...], (1, 0))[0:heads]
        st_tx[st, heads : 2 * heads] = jnp.transpose(stl[...], (1, 0))[0:heads]
        for i in range(1, n_ka):
            st_copy(st, i).start()

    def finish(st):
        for i in range(1, n_ka):
            st_copy(st, i).wait_recv()
        tops = [st_tx[st, 0:heads]] + [st_rx[st, i, 0:heads] for i in range(1, n_ka)]
        sums = [st_tx[st, heads : 2 * heads]] + [st_rx[st, i, heads : 2 * heads] for i in range(1, n_ka)]
        top = functools.reduce(jnp.maximum, tops)
        total = functools.reduce(
            jnp.add, [b * jnp.exp2((a - top) * scale_main) for a, b in zip(tops, sums)]
        )
        comb[0:heads] = top
        comb[heads : 2 * heads] = 1.0 / (total * main_total)
        cols = jnp.transpose(comb[...], (1, 0))
        for head in range(heads):
            gtop = jnp.broadcast_to(cols[:, head : head + 1], (rows, LANES))
            ginv = jnp.broadcast_to(cols[:, heads + head : heads + head + 1], (rows, LANES))
            f_ref[st, head] = jnp.exp2((f_ref[st, head] - gtop) * scale_main) * ginv

        def one(g, carry):
            at = pl.ds(pl.multiple_of(g * 8, 8), 8)
            acc = [jnp.zeros((8, LANES), jnp.float32) for _ in range(tiles)]
            for head in range(heads):
                f = f_ref[st, head, at, :]
                slot = eslot(st, head)
                for c in range(tiles):
                    acc[c] = acc[c] + f * e_ref[slot, at, c * LANES : (c + 1) * LANES]
            spot = st * half + g // 4
            to = pl.ds(pl.multiple_of(lax.rem(g, 4) * 8, 8), 8)
            for c in range(tiles):
                part, inner = divmod(c, tiles // 2)
                t_ref[spot, part, to, inner * LANES : (inner + 1) * LANES] = acc[c]
            return carry

        lax.fori_loop(0, groups, one, 0)

    def spot_of(offset):
        return offsets.index(offset)

    def ra_copy(a, c):
        src = t_ref.at[spot_of(half if a == 0 else -(half - a)), c]
        return copy_to(src, rxa.at[a, c], ra_s.at[a, c], ra_r.at[a, c], ha_dev(-1))

    def rb_copy(a, c):
        src = t_ref.at[spot_of(half - a), c]
        return copy_to(src, rxb.at[a, c], rb_s.at[a, c], rb_r.at[a, c], ha_dev(1))

    def chain_a(a, c):
        if a > 1 or (a == 1 and c == 0):
            ra_copy(a - 1, c).wait_recv()
            spot = spot_of(-(half - a))
            t_ref[spot, c] = t_ref[spot, c] + rxa[a - 1, c]
        ra_copy(a, c).start()

    def chain_b(a, c):
        if a > 1 or (a == 1 and c == 1):
            rb_copy(a - 1, c).wait_recv()
            spot = spot_of(half - a)
            t_ref[spot, c] = t_ref[spot, c] + rxb[a - 1, c]
        rb_copy(a, c).start()

    def fwd(st, after):
        last = st == 1
        kcopy(0, 0).wait()
        scores(st, 0, 0, s0)
        kcopy(NBUF, 0).start()

        def pair(i, carry):
            h0 = 2 * i
            a = lax.rem(h0 + 1, NBUF)
            b = lax.rem(h0 + 2, NBUF)
            kcopy(h0 + 1, a).wait()
            kcopy(h0 + 2, b).wait()
            scores(st, h0 + 1, a, s1)
            soften(st, h0, s0)
            scores(st, h0 + 2, b, s0)
            soften(st, h0 + 1, s1)

            def refill():
                kcopy(lax.rem(h0 + 1 + NBUF, heads), a).start()
                kcopy(lax.rem(h0 + 2 + NBUF, heads), b).start()

            if last:
                pl.when(h0 + 1 + NBUF < heads)(lambda: kcopy(h0 + 1 + NBUF, a).start())
                pl.when(h0 + 2 + NBUF < heads)(lambda: kcopy(h0 + 2 + NBUF, b).start())
            else:
                refill()
            after(i)
            return carry

        lax.fori_loop(0, heads // 2 - 1, pair, 0)
        end = (heads - 1) % NBUF
        kcopy(heads - 1, end).wait()
        scores(st, heads - 1, end, s1)
        if not last:
            kcopy(NBUF - 1, end).start()
        soften(st, heads - 2, s0)
        soften(st, heads - 1, s1)

    fwd(0, lambda i: None)
    send_stats(0)

    def beside(i):
        @pl.when(i == EXTRA // 2 - 1)
        def _():
            finish(0)
            chain_a(0, 0)
            chain_b(0, 1)
            chain_a(1, 1)
            chain_b(1, 0)

        @pl.when(i == EXTRA // 2 + 1)
        def _():
            chain_a(1, 0)
            chain_b(1, 1)

        @pl.when(i == EXTRA // 2 + 3)
        def _():
            chain_a(2, 1)
            chain_a(2, 0)

    fwd(1, beside)
    send_stats(1)

    iq_all[:, pl.ds(pl.multiple_of(h * 64, 64), 64), :] = iq_ref[:, pl.ds(pl.multiple_of(h * 64, 64), 64), :]
    wc_all[h] = wc_ref[h]
    ctx[pl.ds(pl.multiple_of(p * 256, 256), 256), :] = ik_ref[...]
    for i in range(1, n_pb):
        cx_copy(i).wait_recv()
    for i in range(1, n_ha):
        iq_copy(i).wait_recv()
        wc_copy(i).wait_recv()
    ctx_t[...] = jnp.transpose(ctx[...].astype(jnp.float32), (1, 0)).astype(jnp.bfloat16)
    for src in range(n_ha):
        for kk in range(n_ka // 2):
            spread = lane_spread(wc_all[src, kk : kk + 1, :])
            for one in range(2):
                w_rep[2 * kk + one, src * 64 : src * 64 + 64, :] = spread[one * 64 : one * 64 + 64]
    per = n_ha * 64
    for kk in range(n_ka):
        wq = jnp.transpose(w_rep[kk] * iq_all[kk].astype(jnp.float32), (1, 0))
        big = wq.astype(jnp.bfloat16)
        wq_t[0:128, kk * per : (kk + 1) * per] = big
        wq_t[128:256, kk * per : (kk + 1) * per] = (wq - big.astype(jnp.float32)).astype(jnp.bfloat16)

    finish(1)
    for c in range(2):
        chain_b(2, c)

    step = 512

    def index_part(n, carry):
        kk, sc = n // (keys // step), lax.rem(n, keys // step)
        at = pl.ds(pl.multiple_of(sc * step, step), step)
        act = jnp.dot(iq_all[kk], ctx_t[:, at], preferred_element_type=jnp.float32)
        w = w_rep[kk]
        parts = []
        for c in range(step // LANES):
            a = act[:, c * LANES : (c + 1) * LANES]
            r = jnp.maximum(a, 0.0) * w
            parts.append(jnp.sum(jnp.sum(r.reshape(n_ha, 64, LANES), axis=0).reshape(8, 8, LANES), axis=1))
        lg[kk, :, at] = jnp.concatenate(parts, axis=1) * scale
        m_ref[kk, :, at] = jnp.where(act > 0, 1.0, 0.0).astype(jnp.bfloat16)
        return carry

    total_parts = n_ka * (keys // step)
    lax.fori_loop(0, total_parts // 2, index_part, 0)
    for c in range(2):
        chain_a(3, c)
        chain_b(3, c)
    lax.fori_loop(total_parts // 2, total_parts, index_part, 0)

    me = dest_of(n_ha - 1)
    rel = pos_ref[me][:, 0:1] - first_key
    seen = lax.broadcasted_iota(jnp.int32, (32, keys), 1) <= rel
    logits = jnp.where(seen, lg[...].reshape(32, keys), LOW)
    row_top = jnp.max(logits, axis=1, keepdims=True)
    expo = jnp.where(seen, jnp.exp(logits - row_top), 0.0)
    row_sum = jnp.sum(expo, axis=1, keepdims=True)
    lg[...] = expo.reshape(n_ka, 8, keys)
    ix_tx[0] = jnp.broadcast_to(row_top, (32, LANES))
    ix_tx[1] = jnp.broadcast_to(row_sum, (32, LANES))

    def ix_copy(i):
        return copy_to(ix_tx, ix_rx.at[i], ix_s.at[i], ix_r.at[i], ka_dev(i))

    for i in range(1, n_ka):
        ix_copy(i).start()
    for i in range(1, n_ka):
        ix_copy(i).wait_recv()
    tops = [ix_tx[0]] + [ix_rx[i, 0] for i in range(1, n_ka)]
    sums = [ix_tx[1]] + [ix_rx[i, 1] for i in range(1, n_ka)]
    top = functools.reduce(jnp.maximum, tops)
    total = functools.reduce(jnp.add, [b * jnp.exp(a - top) for a, b in zip(tops, sums)])
    factor = (jnp.exp(tops[0] - top) / total)[:, 0:1]

    for c in range(2):
        ra_copy(half - 1, c).wait_recv()
        rb_copy(half - 1, c).wait_recv()
        at = slice(c * (keys // 2), (c + 1) * (keys // 2))
        target = t_ref[n_ha - 1, c] + rxa[half - 1, c] + rxb[half - 1, c]
        diff = (lg[:, :, at].reshape(32, keys // 2) * factor - target) * (key_total / 16.0)
        big = diff.astype(jnp.bfloat16).astype(jnp.float32)
        small = diff - big
        for t in range(32):
            kk, r = divmod(t, 8)
            if r % 2:
                continue
            for value, ref in ((big, d_hi), (small, d_lo)):
                both = jnp.concatenate(
                    [
                        jnp.broadcast_to(value[t : t + 1], (8, keys // 2)),
                        jnp.broadcast_to(value[t + 1 : t + 2], (8, keys // 2)),
                    ],
                    axis=0,
                )
                ref[kk, r * 8 : r * 8 + 16, at] = both.astype(jnp.bfloat16)

    u_ref[...] = jnp.zeros_like(u_ref)

    def gk_copy(i):
        return copy_to(gk_tx.at[i], gk_rx.at[i], gk_s.at[i], gk_r.at[i], pb_dev(i))

    def back(n, carry):
        i = n + 1
        dest = lax.rem(p + i, n_pb)
        at = pl.ds(pl.multiple_of(dest * 256, 256), 256)
        key = ctx[at, :]
        wide = jnp.zeros((256, 256), jnp.float32)
        thin = jnp.zeros((128, 256), jnp.float32)
        for kk in range(n_ka):
            mask = m_ref[kk, :, at].reshape(n_ha, 64, 256)
            hi = (mask * d_hi[kk, :, at][None]).reshape(per, 256)
            lo = (mask * d_lo[kk, :, at][None]).reshape(per, 256)
            u_ref[kk] = u_ref[kk] + (
                jnp.dot(hi, key, preferred_element_type=jnp.float32)
                + jnp.dot(lo, key, preferred_element_type=jnp.float32)
            )
            wide += jnp.dot(wq_t[:, kk * per : (kk + 1) * per], hi, preferred_element_type=jnp.float32)
            thin += jnp.dot(wq_t[0:128, kk * per : (kk + 1) * per], lo, preferred_element_type=jnp.float32)
        block = (wide[0:128] + wide[128:256] + thin) * scale
        gk_tx[lax.rem(i, n_pb)] = jnp.transpose(block, (1, 0))

        @pl.when(i < n_pb)
        def _():
            gk_copy(i).start()

        return carry

    lax.fori_loop(0, n_pb, back, 0)

    core, far = lax.rem(k, 2), k // 2

    def u_copy(x):
        return copy_to(
            u_ref.at[x * 2 + 1 - core], u_rx.at[x], u_s.at[x], u_r.at[x], {"ka": far * 2 + 1 - core}
        )

    for x in range(2):
        u_copy(x).start()
    for x in range(2):
        u_copy(x).wait_recv()
        v_ref[x] = u_ref[x * 2 + core] + u_rx[x]
    v_copy = copy_to(v_ref.at[1 - far], v_rx, v_s.at[0], v_r.at[0], {"ka": (1 - far) * 2 + core})
    v_copy.start()

    own = gk_tx[0]
    for i in range(1, n_pb):
        gk_copy(i).wait_recv()
        own = own + gk_rx[i]
    z_tx[...] = own.reshape(n_ha, 256 // n_ha, 128)

    def z_copy(i):
        return copy_to(z_tx.at[lax.rem(h + i, n_ha)], z_rx.at[i], z_s.at[i], z_r.at[i], ha_dev(i))

    for i in range(1, n_ha):
        z_copy(i).start()

    v_copy.wait_recv()
    r_ref[...] = (v_ref[far] + v_rx[...]) * scale

    def o_copy(i):
        dest = lax.rem(h + i, n_ha)
        return copy_to(
            r_ref.at[pl.ds(pl.multiple_of(dest * 64, 64), 64), :], o_rx.at[h], o_s.at[i], o_r.at[i], ha_dev(i)
        )

    for i in range(1, n_ha):
        o_copy(i).start()

    mine = z_tx[h]
    for i in range(1, n_ha):
        z_copy(i).wait_recv()
        mine = mine + z_rx[i]
    zsum[h] = mine

    def y_copy(i):
        return copy_to(zsum.at[h], zsum.at[h], y_s.at[i], y_r.at[i], ha_dev(i))

    for i in range(1, n_ha):
        y_copy(i).start()

    o_rx[h] = r_ref[pl.ds(pl.multiple_of(h * 64, 64), 64), :]
    for i in range(1, n_ha):
        o_copy(i).wait_recv()
    own_rows = pl.ds(pl.multiple_of(k * 4, 4), 4)
    per_row = wn_ref[own_rows, :]
    for b in range(4):
        at = slice(b * LANES, (b + 1) * LANES)
        u = o_rx[2 * b : 2 * b + 2].reshape(LANES, 128)
        gq_ref[at, :] = u * lane_spread(per_row[b : b + 1])
        dots = jnp.transpose(u * iq_ref[k, at, :].astype(jnp.float32), (1, 0))
        gw_ref[:, at] = jnp.broadcast_to(jnp.sum(dots, axis=0, keepdims=True), (8, LANES))

    for i in range(1, n_ha):
        y_copy(i).wait_recv()
    gk_ref[...] = zsum[...].reshape(256, 128)

    for i in range(1, n_pb):
        cx_copy(i).wait_send()
        gk_copy(i).wait_send()
    for i in range(1, n_ha):
        iq_copy(i).wait_send()
        wc_copy(i).wait_send()
        z_copy(i).wait_send()
        o_copy(i).wait_send()
        y_copy(i).wait_send()
    for i in range(1, n_ka):
        for st in range(2):
            st_copy(st, i).wait_send()
        ix_copy(i).wait_send()
    for a in range(half):
        for c in range(2):
            if a or c == 0:
                ra_copy(a, c).wait_send()
            if a or c == 1:
                rb_copy(a, c).wait_send()
    for x in range(2):
        u_copy(x).wait_send()
    v_copy.wait_send()


def body(sizes, main_query, main_key, index_query, index_weight, index_key, query_pos):
    n_pb, n_ha, n_ka = sizes
    t, heads, dh = main_query.shape
    keys = main_key.shape[0]
    joined = index_query.shape[1]
    dims = (n_pb, n_ha, n_ka, heads, dh, keys, heads * n_ha, keys * n_ka)
    q = main_query.reshape(n_ka, n_ha, 8, heads, dh).transpose(3, 1, 0, 2, 4).reshape(heads, n_ha, 32, dh)
    kt = main_key.transpose(1, 2, 0)
    pos = query_pos.reshape(n_ka, n_ha, 8).transpose(1, 0, 2).reshape(n_ha, 32, 1)
    pos = jnp.broadcast_to(pos, (n_ha, 32, LANES))
    iq = index_query.reshape(n_ka, n_ha * 64, 128)
    wide = index_weight.astype(jnp.float32)
    wc = wide.reshape(n_ka, n_ha, 64).transpose(1, 0, 2).reshape(n_ha, n_ka * 64 // LANES, LANES)
    wc = jnp.pad(wc, ((0, 0), (0, 8 - wc.shape[1]), (0, 0)))
    wn = wide.reshape(t * joined // LANES, LANES)

    half = n_ha // 2
    rows = half * 32
    per = n_ha * 64
    f32, bf16 = jnp.float32, jnp.bfloat16
    scratch = [
        pltpu.VMEM((NBUF, dh, keys), bf16),
        pltpu.VMEM((rows, keys), f32),
        pltpu.VMEM((rows, keys), f32),
        pltpu.VMEM((heads + EXTRA, rows, keys), f32),
        pltpu.VMEM((2, heads, rows, LANES), f32),
        pltpu.VMEM((rows, LANES), f32),
        pltpu.VMEM((rows, LANES), f32),
        pltpu.VMEM((2, 2 * heads, rows), f32),
        pltpu.VMEM((2, n_ka, 2 * heads, rows), f32),
        pltpu.VMEM((LANES, rows), f32),
        pltpu.VMEM((n_ha, 2, 32, keys // 2), f32),
        pltpu.VMEM((half, 2, 32, keys // 2), f32),
        pltpu.VMEM((half, 2, 32, keys // 2), f32),
        pltpu.VMEM((n_ka, per, 128), bf16),
        pltpu.VMEM((n_ha, 8, LANES), f32),
        pltpu.VMEM((n_ka, per, LANES), f32),
        pltpu.VMEM((256, n_ka * per), bf16),
        pltpu.VMEM((keys, 128), bf16),
        pltpu.VMEM((128, keys), bf16),
        pltpu.VMEM((n_ka, per, keys), bf16),
        pltpu.VMEM((n_ka, 8, keys), f32),
        pltpu.VMEM((n_ka, 64, keys), bf16),
        pltpu.VMEM((n_ka, 64, keys), bf16),
        pltpu.VMEM((2, 32, LANES), f32),
        pltpu.VMEM((n_ka, 2, 32, LANES), f32),
        pltpu.VMEM((n_ka, per, 128), f32),
        pltpu.VMEM((2, per, 128), f32),
        pltpu.VMEM((2, per, 128), f32),
        pltpu.VMEM((per, 128), f32),
        pltpu.VMEM((per, 128), f32),
        pltpu.VMEM((n_ha, 64, 128), f32),
        pltpu.VMEM((n_pb, 256, 128), f32),
        pltpu.VMEM((n_pb, 256, 128), f32),
        pltpu.VMEM((n_ha, 256 // n_ha, 128), f32),
        pltpu.VMEM((n_ha, 256 // n_ha, 128), f32),
        pltpu.VMEM((n_ha, 256 // n_ha, 128), f32),
    ]
    dma = pltpu.SemaphoreType.DMA
    sems = [dma((NBUF,))]
    for shape in (
        (2, n_ka), (half, 2), (half, 2), (n_ha,), (n_ha,), (n_pb,),
        (n_ka,), (2,), (1,), (n_ha,), (n_pb,), (n_ha,), (n_ha,),
    ):
        sems += [dma(shape), dma(shape)]
    vmem = pl.BlockSpec(memory_space=pltpu.VMEM)
    gq, gw, gk = pl.pallas_call(
        functools.partial(kernel, dims),
        out_shape=(
            jax.ShapeDtypeStruct((per, 128), f32),
            jax.ShapeDtypeStruct((8, per), f32),
            jax.ShapeDtypeStruct((256, 128), f32),
        ),
        in_specs=[vmem, pl.BlockSpec(memory_space=pl.ANY)] + [vmem] * 5,
        out_specs=(vmem, vmem, vmem),
        scratch_shapes=scratch + sems,
        compiler_params=pltpu.CompilerParams(
            collective_id=0, has_side_effects=True, vmem_limit_bytes=63 * 1024 * 1024
        ),
    )(q, kt, pos, iq, wc, wn, index_key)
    return (gq.reshape(t // n_ka, joined, 128), gw[0].reshape(t // n_ka, joined), gk)


def solution(mesh):
    placed = (
        P("pb", "ha", None),
        P("ka", "ha", None),
        P("pb", "ha", None),
        P("pb", "ha"),
        P(("pb", "ka"), None),
        P("pb"),
    )
    sizes = tuple(mesh.shape[name] for name in ("pb", "ha", "ka"))
    return jax.shard_map(
        functools.partial(body, sizes),
        mesh=mesh,
        in_specs=placed,
        out_specs=(P(("pb", "ka"), "ha", None), P(("pb", "ka"), "ha"), P(("pb", "ka"), None)),
        check_vma=False,
    )
```

time: 476 us -> 108 us (0.23)
  waiting for transfers between devices: 272 us -> 0 us
  Pallas kernels: 0 us -> 94 us
  matrix products: 63.3 us -> 0 us
  other arithmetic: 58.5 us -> 0 us
  blocking collectives: 56.3 us -> 0 us
  between operations: 13.9 us -> 0.7 us
    psum x2 -> x0, waiting for transfers between devices: 184 us -> none  [the longest x1 112 us: body(): target, logits = lax.psum((target_part, logit_part), 'ha')]
    pallas_call x0 -> x1, Pallas kernels: none -> 94 us  [body(): pl.pallas_call(functools.partial(kernel, dims), out_shape=(jax.ShapeDtype...]
    dot_general x4 -> x0, matrix products: 63.3 us -> none  [the longest x1 19.6 us: body(): jnp.einsum('thd,shd->hts', main_query, main_key, preferred_element_type=j...]
    all_gather x5 -> x0, blocking collectives: 56.3 us -> none  [the longest x1 29.7 us: body(): ctx_key = lax.all_gather(index_key, 'pb', axis=0, tiled=True)]
    reduce_scatter x2 -> x0, waiting for transfers between devices: 51.6 us -> none  [the longest x1 37.9 us: body(): lax.psum_scatter(query_part, 'ka', scatter_dimension=0, tiled=True)]
    unnamed x6 -> x0, waiting for transfers between devices: 35.9 us -> none
    reduce_sum x4 -> x0, other arithmetic: 35.6 us -> none  [the longest x2 17.5 us: local_stats(): return (maxima, expos, jnp.sum(expos, axis=-1))]
    unnamed x2 -> x0, other arithmetic: 17.2 us -> none
  transfers between devices with their start and end apart: 5 -> 0, of which waited for: 5 -> 0; matrix products, arithmetic and copies ran while one was open for 6% -> 0% of each run, Pallas kernels for 0% -> 0%
where the time goes in v1:
time: 108 us; the launch traced here: 107 us
  Pallas kernels  94 us (87%)
  local copies, waits for them, and re-layouts  12.6 us (12%)
    pallas_call x1, Pallas kernels, body(): pl.pallas_call(functools.partial(kernel, dims), out_shape=(jax.ShapeDtype...  94 us
    unnamed x8, local copies, waits for them, and re-layouts  7.15 us

profile of v1, /device:TPU:8, one launch (start us, length us, event | category | flops | bytes accessed | tf_op | source)
XLA Modules:
  0.0 107.3 jit_solution(1392902320715969411)
XLA Ops:
  0.6 3.2 %copy.18 = bf16[256,16,192]{2,1,0:T(8,128)(2,1)S(1)} copy(bf16[256,16,192]{0,2,1:T(8,128)(2,1)} %param.6) | data formatting | bytes 3145728 | tf_op args[0]
  3.9 0.0 copy-start.1
  3.9 0.0 copy-start
  3.9 2.1 %copy.26 = bf16[16,8,4,8,192]{4,3,2,1,0:T(8,128)(2,1)} copy(bf16[16,8,4,8,192]{4,0,3,1,2:T(8,128)(2,1)S(1)} %bitcast.13) | data formatting | bytes 3145728 | tf_op jit(solution)/shard_map/transpose | solution.py:497
  6.0 0.0 copy-done.1
  6.0 0.1 reshape.34
  6.1 0.1 broadcast_in_dim.7
  6.1 0.8 broadcast_in_dim.8.pos_ref
  6.9 0.0 copy-done
  6.9 0.1 copy.21
  7.0 0.1 reshape.36
  7.1 0.1 reshape.37
  7.2 0.6 pad.4.wc_ref
  7.8 0.7 reshape.38.wn_ref
  8.5 94.0 %shard_map.85 = (f32[512,128]{1,0:T(8,128)}, f32[8,512]{1,0:T(8,128)}, f32[256,128]{1,0:T(8,128)}) custom-call(bf16[16,8,32,192]{3,2,1,0:T(8,128)(2,1)} %bitcast.12, bf16[16,192,2048]{2,1,0:T(8,128)(2,1)} %bitcast.11, s32[8,32,128]{2,1,0:T(8,128)} %broadcast_in_dim.8.pos_ref, bf16[4,512,128]{2,1,0:T(8,128)(2,1)} %bitcast.14, f32[8,8,128]{2,1,0:T(8,128)} %pad.4.wc_ref, ...), custom_call_target="tpu_custom_call" | custom-call | tf_op jit(solution)/shard_map/pallas_call | solution.py:557
  102.6 0.7 slice_reduce_fusion
  103.3 0.1 reshape_squeeze.3
  103.4 0.7 copy.24
  104.1 1.7 %copy.29 = f32[64,8,128]{2,1,0:T(8,128)} copy(f32[64,8,128]{2,1,0:T(8,128)} %bitcast.15) | data formatting | bytes 524288
  105.7 1.6 %copy.30 = f32[256,128]{1,0:T(8,128)} copy(f32[256,128]{1,0:T(8,128)} %get-tuple-element.23) | data formatting | bytes 262144
  (2 shorter events, 0.0 us)
Async XLA Ops:
  3.9 2.1 %copy-start.1 = (s32[256]{0:T(256)S(1)}, s32[256]{0:T(256)}, u32[]{:S(2)}) copy-start(s32[256]{0:T(256)} %param.11) | copy-start | bytes 3076
  3.9 3.0 %copy-start = (bf16[256,8]{0,1:T(8,128)(2,1)S(1)}, bf16[256,8]{0,1:T(8,128)(2,1)}, u32[]{:S(2)}) copy-start(bf16[256,8]{0,1:T(8,128)(2,1)} %param.9) | copy-start | bytes 12292

commit v2 on v1

--- a/solution.py
+++ b/solution.py
@@ -22,9 +22,9 @@
 
 def kernel(
     dims,
-    q_ref, kt_ref, pos_ref, iq_ref, wc_ref, wn_ref, ik_ref,
+    qt_ref, kt_ref, iq_ref, wc_ref, ik_ref,
     gq_ref, gw_ref, gk_ref,
-    kbuf, s0, s1, e_ref, f_ref, stm, stl, st_tx, st_rx, comb,
+    q_ref, q_wide, pos_ref, w_own, kbuf, s0, s1, e_ref, f_ref, stm, stl, st_tx, st_rx, comb,
     t_ref, rxa, rxb,
     iq_all, wc_all, w_rep, wq_t, ctx, ctx_t, m_ref, lg, d_hi, d_lo,
     ix_tx, ix_rx,
@@ -75,8 +75,6 @@
         pl.semaphore_signal(barrier, inc=1, device_id=pb_dev(i), device_id_type=MESH)
     for i in range(1, n_ka):
         pl.semaphore_signal(barrier, inc=1, device_id=ka_dev(i), device_id_type=MESH)
-    pl.semaphore_wait(barrier, n_ha + n_pb + n_ka - 3)
-
     def iq_copy(i):
         dest = lax.rem(h + i, n_ha)
         return copy_to(
@@ -94,11 +92,13 @@
             ik_ref, ctx.at[pl.ds(pl.multiple_of(p * 256, 256), 256), :], cx_s.at[i], cx_r.at[i], pb_dev(i)
         )
 
-    for i in range(1, n_pb):
-        cx_copy(i).start()
-    for i in range(1, n_ha):
-        iq_copy(i).start()
-        wc_copy(i).start()
+    def greet():
+        pl.semaphore_wait(barrier, n_ha + n_pb + n_ka - 3)
+        for i in range(1, n_pb):
+            cx_copy(i).start()
+        for i in range(1, n_ha):
+            iq_copy(i).start()
+            wc_copy(i).start()
 
     lane = lax.broadcasted_iota(jnp.int32, (8, LANES), 1)
     lane_rows = lax.broadcasted_iota(jnp.int32, (rows, LANES), 1)
@@ -107,8 +107,22 @@
     def dest_of(i):
         return lax.rem(h + offsets[i] + n_ha, n_ha)
 
+    for i in range(n_ha):
+        pos_ref[i] = lane_spread(wc_ref[dest_of(i), 2:3, :])[0:32].astype(jnp.int32)
+
+    def order_queries(head, carry):
+        q_wide[...] = jnp.transpose(qt_ref[head].astype(jnp.float32), (1, 0))
+        for i in range(n_ha):
+            chunk = [
+                q_wide[pl.ds(pl.multiple_of(kk * n_ha * 8 + dest_of(i) * 8, 8), 8), :] for kk in range(n_ka)
+            ]
+            q_ref[head, i * 32 : i * 32 + 32, :] = jnp.concatenate(chunk, axis=0).astype(jnp.bfloat16)
+        return carry
+
+    lax.fori_loop(0, heads, order_queries, 0)
+
     def scores(st, head, slot, out):
-        q = jnp.concatenate([q_ref[head, dest_of(st * half + i)] for i in range(half)], axis=0)
+        q = q_ref[head, st * rows : (st + 1) * rows, :]
         out[...] = jnp.dot(q, kbuf[slot], preferred_element_type=jnp.float32)
 
     def eslot(st, head):
@@ -118,7 +132,7 @@
         slot = eslot(st, head)
         tops, sums = [], []
         for g in range(groups):
-            rel = pos_ref[dest_of(st * half + g // 4), pl.ds((g % 4) * 8, 8), :] - first_key - lane
+            rel = pos_ref[st * half + g // 4, (g % 4) * 8 : (g % 4) * 8 + 8, :] - first_key - lane
             x = [
                 jnp.where(rel >= c * LANES, src[g * 8 : g * 8 + 8, c * LANES : (c + 1) * LANES], LOW)
                 for c in range(tiles)
@@ -207,7 +221,7 @@
             t_ref[spot, c] = t_ref[spot, c] + rxb[a - 1, c]
         rb_copy(a, c).start()
 
-    def fwd(st, after):
+    def fwd(st, after, early):
         last = st == 1
         kcopy(0, 0).wait()
         scores(st, 0, 0, s0)
@@ -236,7 +250,12 @@
             after(i)
             return carry
 
-        lax.fori_loop(0, heads // 2 - 1, pair, 0)
+        if last:
+            lax.fori_loop(0, heads // 2 - 1, pair, 0)
+        else:
+            lax.fori_loop(0, 1, pair, 0)
+            early()
+            lax.fori_loop(1, heads // 2 - 1, pair, 0)
         end = (heads - 1) % NBUF
         kcopy(heads - 1, end).wait()
         scores(st, heads - 1, end, s1)
@@ -245,7 +264,7 @@
         soften(st, heads - 2, s0)
         soften(st, heads - 1, s1)
 
-    fwd(0, lambda i: None)
+    fwd(0, lambda i: None, greet)
     send_stats(0)
 
     def beside(i):
@@ -267,7 +286,7 @@
             chain_a(2, 1)
             chain_a(2, 0)
 
-    fwd(1, beside)
+    fwd(1, beside, None)
     send_stats(1)
 
     iq_all[:, pl.ds(pl.multiple_of(h * 64, 64), 64), :] = iq_ref[:, pl.ds(pl.multiple_of(h * 64, 64), 64), :]
@@ -284,6 +303,8 @@
             spread = lane_spread(wc_all[src, kk : kk + 1, :])
             for one in range(2):
                 w_rep[2 * kk + one, src * 64 : src * 64 + 64, :] = spread[one * 64 : one * 64 + 64]
+        spread = lane_spread(wc_ref[src, pl.ds(k // 2, 1), :])
+        w_own[src * 64 : src * 64 + 64, :] = jnp.where(lax.rem(k, 2) == 0, spread[0:64], spread[64:128])
     per = n_ha * 64
     for kk in range(n_ka):
         wq = jnp.transpose(w_rep[kk] * iq_all[kk].astype(jnp.float32), (1, 0))
@@ -318,8 +339,7 @@
         chain_b(3, c)
     lax.fori_loop(total_parts // 2, total_parts, index_part, 0)
 
-    me = dest_of(n_ha - 1)
-    rel = pos_ref[me][:, 0:1] - first_key
+    rel = pos_ref[n_ha - 1][:, 0:1] - first_key
     seen = lax.broadcasted_iota(jnp.int32, (32, keys), 1) <= rel
     logits = jnp.where(seen, lg[...].reshape(32, keys), LOW)
     row_top = jnp.max(logits, axis=1, keepdims=True)
@@ -364,26 +384,21 @@
                 )
                 ref[kk, r * 8 : r * 8 + 16, at] = both.astype(jnp.bfloat16)
 
-    u_ref[...] = jnp.zeros_like(u_ref)
-
     def gk_copy(i):
         return copy_to(gk_tx.at[i], gk_rx.at[i], gk_s.at[i], gk_r.at[i], pb_dev(i))
 
-    def back(n, carry):
+    def gated(kk, at, width, d_ref):
+        return (m_ref[kk, :, at].reshape(n_ha, 64, width) * d_ref[kk, :, at][None]).reshape(per, width)
+
+    def key_block(n, carry):
         i = n + 1
         dest = lax.rem(p + i, n_pb)
         at = pl.ds(pl.multiple_of(dest * 256, 256), 256)
-        key = ctx[at, :]
         wide = jnp.zeros((256, 256), jnp.float32)
         thin = jnp.zeros((128, 256), jnp.float32)
         for kk in range(n_ka):
-            mask = m_ref[kk, :, at].reshape(n_ha, 64, 256)
-            hi = (mask * d_hi[kk, :, at][None]).reshape(per, 256)
-            lo = (mask * d_lo[kk, :, at][None]).reshape(per, 256)
-            u_ref[kk] = u_ref[kk] + (
-                jnp.dot(hi, key, preferred_element_type=jnp.float32)
-                + jnp.dot(lo, key, preferred_element_type=jnp.float32)
-            )
+            hi = gated(kk, at, 256, d_hi)
+            lo = gated(kk, at, 256, d_lo)
             wide += jnp.dot(wq_t[:, kk * per : (kk + 1) * per], hi, preferred_element_type=jnp.float32)
             thin += jnp.dot(wq_t[0:128, kk * per : (kk + 1) * per], lo, preferred_element_type=jnp.float32)
         block = (wide[0:128] + wide[128:256] + thin) * scale
@@ -395,22 +410,50 @@
 
         return carry
 
-    lax.fori_loop(0, n_pb, back, 0)
-
     core, far = lax.rem(k, 2), k // 2
+
+    def query_rows(kk):
+        def block(n, total):
+            at = pl.ds(pl.multiple_of(n * 512, 512), 512)
+            key = ctx[at, :]
+            return total + (
+                jnp.dot(gated(kk, at, 512, d_hi), key, preferred_element_type=jnp.float32)
+                + jnp.dot(gated(kk, at, 512, d_lo), key, preferred_element_type=jnp.float32)
+            )
+
+        u_ref[kk] = lax.fori_loop(0, keys // 512, block, jnp.zeros((per, 128), jnp.float32))
 
     def u_copy(x):
         return copy_to(
             u_ref.at[x * 2 + 1 - core], u_rx.at[x], u_s.at[x], u_r.at[x], {"ka": far * 2 + 1 - core}
         )
 
+    v_copy = copy_to(v_ref.at[1 - far], v_rx, v_s.at[0], v_r.at[0], {"ka": (1 - far) * 2 + core})
+    early_blocks = n_pb // 2
+    lax.fori_loop(0, early_blocks, key_block, 0)
     for x in range(2):
+        query_rows(x * 2 + 1 - core)
         u_copy(x).start()
-    for x in range(2):
+    for first in range(2):
+        x = 1 - far if first == 0 else far
+        query_rows(x * 2 + core)
         u_copy(x).wait_recv()
         v_ref[x] = u_ref[x * 2 + core] + u_rx[x]
-    v_copy = copy_to(v_ref.at[1 - far], v_rx, v_s.at[0], v_r.at[0], {"ka": (1 - far) * 2 + core})
-    v_copy.start()
+        if first == 0:
+            v_copy.start()
+    lax.fori_loop(early_blocks, n_pb, key_block, 0)
+
+    v_copy.wait_recv()
+    r_ref[...] = (v_ref[far] + v_rx[...]) * scale
+
+    def o_copy(i):
+        dest = lax.rem(h + i, n_ha)
+        return copy_to(
+            r_ref.at[pl.ds(pl.multiple_of(dest * 64, 64), 64), :], o_rx.at[h], o_s.at[i], o_r.at[i], ha_dev(i)
+        )
+
+    for i in range(1, n_ha):
+        o_copy(i).start()
 
     own = gk_tx[0]
     for i in range(1, n_pb):
@@ -424,18 +467,6 @@
     for i in range(1, n_ha):
         z_copy(i).start()
 
-    v_copy.wait_recv()
-    r_ref[...] = (v_ref[far] + v_rx[...]) * scale
-
-    def o_copy(i):
-        dest = lax.rem(h + i, n_ha)
-        return copy_to(
-            r_ref.at[pl.ds(pl.multiple_of(dest * 64, 64), 64), :], o_rx.at[h], o_s.at[i], o_r.at[i], ha_dev(i)
-        )
-
-    for i in range(1, n_ha):
-        o_copy(i).start()
-
     mine = z_tx[h]
     for i in range(1, n_ha):
         z_copy(i).wait_recv()
@@ -451,12 +482,10 @@
     o_rx[h] = r_ref[pl.ds(pl.multiple_of(h * 64, 64), 64), :]
     for i in range(1, n_ha):
         o_copy(i).wait_recv()
-    own_rows = pl.ds(pl.multiple_of(k * 4, 4), 4)
-    per_row = wn_ref[own_rows, :]
     for b in range(4):
         at = slice(b * LANES, (b + 1) * LANES)
         u = o_rx[2 * b : 2 * b + 2].reshape(LANES, 128)
-        gq_ref[at, :] = u * lane_spread(per_row[b : b + 1])
+        gq_ref[at, :] = u * w_own[at, :]
         dots = jnp.transpose(u * iq_ref[k, at, :].astype(jnp.float32), (1, 0))
         gw_ref[:, at] = jnp.broadcast_to(jnp.sum(dots, axis=0, keepdims=True), (8, LANES))
 
@@ -494,21 +523,24 @@
     keys = main_key.shape[0]
     joined = index_query.shape[1]
     dims = (n_pb, n_ha, n_ka, heads, dh, keys, heads * n_ha, keys * n_ka)
-    q = main_query.reshape(n_ka, n_ha, 8, heads, dh).transpose(3, 1, 0, 2, 4).reshape(heads, n_ha, 32, dh)
+    qt = main_query.transpose(1, 2, 0)
     kt = main_key.transpose(1, 2, 0)
-    pos = query_pos.reshape(n_ka, n_ha, 8).transpose(1, 0, 2).reshape(n_ha, 32, 1)
-    pos = jnp.broadcast_to(pos, (n_ha, 32, LANES))
     iq = index_query.reshape(n_ka, n_ha * 64, 128)
-    wide = index_weight.astype(jnp.float32)
-    wc = wide.reshape(n_ka, n_ha, 64).transpose(1, 0, 2).reshape(n_ha, n_ka * 64 // LANES, LANES)
-    wc = jnp.pad(wc, ((0, 0), (0, 8 - wc.shape[1]), (0, 0)))
-    wn = wide.reshape(t * joined // LANES, LANES)
+    wc = index_weight.astype(jnp.float32).reshape(n_ka, n_ha, 64).transpose(1, 0, 2)
+    wc = wc.reshape(n_ha, n_ka * 64 // LANES, LANES)
+    pos = query_pos.astype(jnp.float32).reshape(n_ka, n_ha, 8).transpose(1, 0, 2).reshape(n_ha, 1, 32)
+    pos = jnp.pad(pos, ((0, 0), (0, 7 - wc.shape[1]), (0, LANES - 32)))
+    wc = jnp.concatenate([wc, pos], axis=1)
 
     half = n_ha // 2
     rows = half * 32
     per = n_ha * 64
     f32, bf16 = jnp.float32, jnp.bfloat16
     scratch = [
+        pltpu.VMEM((heads, t, dh), bf16),
+        pltpu.VMEM((t, dh), f32),
+        pltpu.VMEM((n_ha, 32, LANES), jnp.int32),
+        pltpu.VMEM((per, LANES), f32),
         pltpu.VMEM((NBUF, dh, keys), bf16),
         pltpu.VMEM((rows, keys), f32),
         pltpu.VMEM((rows, keys), f32),
@@ -561,13 +593,13 @@
             jax.ShapeDtypeStruct((8, per), f32),
             jax.ShapeDtypeStruct((256, 128), f32),
         ),
-        in_specs=[vmem, pl.BlockSpec(memory_space=pl.ANY)] + [vmem] * 5,
+        in_specs=[vmem, pl.BlockSpec(memory_space=pl.ANY)] + [vmem] * 3,
         out_specs=(vmem, vmem, vmem),
         scratch_shapes=scratch + sems,
         compiler_params=pltpu.CompilerParams(
             collective_id=0, has_side_effects=True, vmem_limit_bytes=63 * 1024 * 1024
         ),
-    )(q, kt, pos, iq, wc, wn, index_key)
+    )(qt, kt, iq, wc, index_key)
     return (gq.reshape(t // n_ka, joined, 128), gw[0].reshape(t // n_ka, joined), gk)
 
 

time: 108 us -> 101 us (0.935)
  local copies, waits for them, and re-layouts: 12.6 us -> 5.88 us
  other arithmetic: 0 us -> 1.31 us
    unnamed x8 -> x3, local copies, waits for them, and re-layouts: 7.15 us -> 3.9 us
    transpose x3 -> x1, local copies, waits for them, and re-layouts: 2.07 us -> 0.01 us  [body(): query_pos.astype(jnp.float32).reshape(n_ka, n_ha, 8).transpose(1, 0, 2)]
where the time goes in v2:
time: 101 us
  Pallas kernels  93.2 us (92%)
  local copies, waits for them, and re-layouts  5.88 us (6%)
  other arithmetic  1.31 us (1%)
    pallas_call x1, Pallas kernels, body(): pl.pallas_call(functools.partial(kernel, dims), out_shape=(jax.ShapeDtype...  93.2 us
    unnamed x3, local copies, waits for them, and re-layouts  3.9 us

profile of v2, /device:TPU:8, one launch (start us, length us, event | category | flops | bytes accessed | tf_op | source)
XLA Modules:
  0.0 101.0 jit_solution(7318649683547573261)
XLA Ops:
  0.6 0.7 convert_element_type.6
  1.3 0.1 reshape.32
  1.4 0.1 reshape.33
  1.5 0.8 copy.10
  2.3 0.1 reshape.39
  2.4 0.1 reshape.36
  2.5 0.6 select_maximum_fusion.wc_ref
  3.1 93.2 %shard_map.85 = (f32[512,128]{1,0:T(8,128)}, f32[8,512]{1,0:T(8,128)}, f32[256,128]{1,0:T(8,128)}) custom-call(bf16[16,192,256]{2,1,0:T(8,128)(2,1)} %bitcast.7, bf16[16,192,2048]{2,1,0:T(8,128)(2,1)} %bitcast.6, bf16[4,512,128]{2,1,0:T(8,128)(2,1)} %bitcast.8, f32[8,8,128]{2,1,0:T(8,128)} %select_maximum_fusion.wc_ref, bf16[256,128]{1,0:T(8,128)(2,1)} %ik_ref.1), custom_call_target="tpu_custom_call" | custom-call | tf_op jit(solution)/shard_map/pallas_call | solution.py:589
  96.3 0.7 slice_reduce_fusion
  97.1 0.1 reshape_squeeze.3
  97.1 0.7 copy.13
  97.8 1.7 %copy.16 = f32[64,8,128]{2,1,0:T(8,128)} copy(f32[64,8,128]{2,1,0:T(8,128)} %bitcast.9) | data formatting | bytes 524288
  99.5 1.6 %copy.17 = f32[256,128]{1,0:T(8,128)} copy(f32[256,128]{1,0:T(8,128)} %get-tuple-element.20) | data formatting | bytes 262144
  (2 shorter events, 0.0 us)

commit v3 on v2

--- a/solution.py
+++ b/solution.py
@@ -14,6 +14,12 @@
 NBUF = 4
 EXTRA = 6
 LOG2E = 1.4426950408889634
+
+
+def stages(n_ha):
+    half = n_ha // 2
+    firsts = (0, half - 1, half + 1, n_ha)
+    return firsts, 32 * max(b - a for a, b in zip(firsts, firsts[1:]))
 
 
 def lane_spread(row):
@@ -36,8 +42,8 @@
     n_pb, n_ha, n_ka, heads, dh, keys, main_total, key_total = dims
     p, h, k = lax.axis_index("pb"), lax.axis_index("ha"), lax.axis_index("ka")
     half = n_ha // 2
-    rows = half * 32
-    groups = rows // 8
+    firsts, most = stages(n_ha)
+    spans = [(firsts[st], firsts[st + 1]) for st in range(len(firsts) - 1)]
     tiles = keys // LANES
     slots = heads + EXTRA
     scale_main = LOG2E / math.sqrt(dh)
@@ -101,7 +107,8 @@
             wc_copy(i).start()
 
     lane = lax.broadcasted_iota(jnp.int32, (8, LANES), 1)
-    lane_rows = lax.broadcasted_iota(jnp.int32, (rows, LANES), 1)
+    for ref in (stm, stl):
+        ref[...] = jnp.zeros_like(ref)
     first_key = k * keys
 
     def dest_of(i):
@@ -122,17 +129,21 @@
     lax.fori_loop(0, heads, order_queries, 0)
 
     def scores(st, head, slot, out):
-        q = q_ref[head, st * rows : (st + 1) * rows, :]
-        out[...] = jnp.dot(q, kbuf[slot], preferred_element_type=jnp.float32)
+        lo, hi = spans[st]
+        q = q_ref[head, lo * 32 : hi * 32, :]
+        out[0 : (hi - lo) * 32] = jnp.dot(q, kbuf[slot], preferred_element_type=jnp.float32)
 
     def eslot(st, head):
         return lax.rem(st * heads + head, slots) if not isinstance(head, int) else (st * heads + head) % slots
 
     def soften(st, head, src):
         slot = eslot(st, head)
+        lo, hi = spans[st]
+        rows = (hi - lo) * 32
+        span = slice(lo * 32, hi * 32)
         tops, sums = [], []
-        for g in range(groups):
-            rel = pos_ref[st * half + g // 4, (g % 4) * 8 : (g % 4) * 8 + 8, :] - first_key - lane
+        for g in range(rows // 8):
+            rel = pos_ref[lo + g // 4, (g % 4) * 8 : (g % 4) * 8 + 8, :] - first_key - lane
             x = [
                 jnp.where(rel >= c * LANES, src[g * 8 : g * 8 + 8, c * LANES : (c + 1) * LANES], LOW)
                 for c in range(tiles)
@@ -147,11 +158,12 @@
             sums.append(total)
         tops = jnp.concatenate(tops, axis=0)
         sums = jnp.concatenate(sums, axis=0)
-        f_ref[st, head] = tops
+        f_ref[head, span] = tops
         row_top = jnp.max(tops, axis=1, keepdims=True)
         row_sum = jnp.sum(sums * jnp.exp2((tops - row_top) * scale_main), axis=1, keepdims=True)
-        stm[...] = jnp.where(lane_rows == head, row_top, stm[...])
-        stl[...] = jnp.where(lane_rows == head, row_sum, stl[...])
+        here = lax.broadcasted_iota(jnp.int32, (rows, LANES), 1) == head
+        stm[span] = jnp.where(here, row_top, stm[span])
+        stl[span] = jnp.where(here, row_sum, stl[span])
 
     def st_copy(st, i):
         return copy_to(st_tx.at[st], st_rx.at[st, i], st_s.at[st, i], st_r.at[st, i], ka_dev(i))
@@ -173,28 +185,31 @@
         )
         comb[0:heads] = top
         comb[heads : 2 * heads] = 1.0 / (total * main_total)
-        cols = jnp.transpose(comb[...], (1, 0))
+        lo, hi = spans[st]
+        rows = (hi - lo) * 32
+        span = slice(lo * 32, hi * 32)
+        cols = jnp.transpose(comb[...], (1, 0))[span]
         for head in range(heads):
             gtop = jnp.broadcast_to(cols[:, head : head + 1], (rows, LANES))
             ginv = jnp.broadcast_to(cols[:, heads + head : heads + head + 1], (rows, LANES))
-            f_ref[st, head] = jnp.exp2((f_ref[st, head] - gtop) * scale_main) * ginv
+            f_ref[head, span] = jnp.exp2((f_ref[head, span] - gtop) * scale_main) * ginv
 
         def one(g, carry):
             at = pl.ds(pl.multiple_of(g * 8, 8), 8)
             acc = [jnp.zeros((8, LANES), jnp.float32) for _ in range(tiles)]
             for head in range(heads):
-                f = f_ref[st, head, at, :]
+                f = f_ref[head, pl.ds(pl.multiple_of(lo * 32 + g * 8, 8), 8), :]
                 slot = eslot(st, head)
                 for c in range(tiles):
                     acc[c] = acc[c] + f * e_ref[slot, at, c * LANES : (c + 1) * LANES]
-            spot = st * half + g // 4
+            spot = lo + g // 4
             to = pl.ds(pl.multiple_of(lax.rem(g, 4) * 8, 8), 8)
             for c in range(tiles):
                 part, inner = divmod(c, tiles // 2)
                 t_ref[spot, part, to, inner * LANES : (inner + 1) * LANES] = acc[c]
             return carry
 
-        lax.fori_loop(0, groups, one, 0)
+        lax.fori_loop(0, rows // 8, one, 0)
 
     def spot_of(offset):
         return offsets.index(offset)
@@ -222,7 +237,7 @@
         rb_copy(a, c).start()
 
     def fwd(st, after, early):
-        last = st == 1
+        last = st == len(spans) - 1
         kcopy(0, 0).wait()
         scores(st, 0, 0, s0)
         kcopy(NBUF, 0).start()
@@ -250,7 +265,7 @@
             after(i)
             return carry
 
-        if last:
+        if early is None:
             lax.fori_loop(0, heads // 2 - 1, pair, 0)
         else:
             lax.fori_loop(0, 1, pair, 0)
@@ -276,18 +291,20 @@
             chain_a(1, 1)
             chain_b(1, 0)
 
-        @pl.when(i == EXTRA // 2 + 1)
+    def beside_last(i):
+        @pl.when(i == 1)
         def _():
             chain_a(1, 0)
             chain_b(1, 1)
 
-        @pl.when(i == EXTRA // 2 + 3)
+        @pl.when(i == EXTRA // 2 - 1)
         def _():
-            chain_a(2, 1)
-            chain_a(2, 0)
+            finish(1)
 
     fwd(1, beside, None)
     send_stats(1)
+    fwd(2, beside_last, None)
+    send_stats(2)
 
     iq_all[:, pl.ds(pl.multiple_of(h * 64, 64), 64), :] = iq_ref[:, pl.ds(pl.multiple_of(h * 64, 64), 64), :]
     wc_all[h] = wc_ref[h]
@@ -312,10 +329,6 @@
         wq_t[0:128, kk * per : (kk + 1) * per] = big
         wq_t[128:256, kk * per : (kk + 1) * per] = (wq - big.astype(jnp.float32)).astype(jnp.bfloat16)
 
-    finish(1)
-    for c in range(2):
-        chain_b(2, c)
-
     step = 512
 
     def index_part(n, carry):
@@ -333,11 +346,15 @@
         return carry
 
     total_parts = n_ka * (keys // step)
-    lax.fori_loop(0, total_parts // 2, index_part, 0)
+    for c in (1, 0):
+        chain_a(2, c)
+        chain_b(2, 1 - c)
+    lax.fori_loop(0, total_parts // 4, index_part, 0)
+    finish(2)
+    lax.fori_loop(total_parts // 4, total_parts, index_part, 0)
     for c in range(2):
         chain_a(3, c)
         chain_b(3, c)
-    lax.fori_loop(total_parts // 2, total_parts, index_part, 0)
 
     rel = pos_ref[n_ha - 1][:, 0:1] - first_key
     seen = lax.broadcasted_iota(jnp.int32, (32, keys), 1) <= rel
@@ -362,7 +379,7 @@
     total = functools.reduce(jnp.add, [b * jnp.exp(a - top) for a, b in zip(tops, sums)])
     factor = (jnp.exp(tops[0] - top) / total)[:, 0:1]
 
-    for c in range(2):
+    def diff_half(c):
         ra_copy(half - 1, c).wait_recv()
         rb_copy(half - 1, c).wait_recv()
         at = slice(c * (keys // 2), (c + 1) * (keys // 2))
@@ -391,8 +408,8 @@
         return (m_ref[kk, :, at].reshape(n_ha, 64, width) * d_ref[kk, :, at][None]).reshape(per, width)
 
     def key_block(n, carry):
-        i = n + 1
-        dest = lax.rem(p + i, n_pb)
+        dest = (n // many) * many + lax.rem(p + n, many)
+        i = lax.rem(dest - p + n_pb, n_pb)
         at = pl.ds(pl.multiple_of(dest * 256, 256), 256)
         wide = jnp.zeros((256, 256), jnp.float32)
         thin = jnp.zeros((128, 256), jnp.float32)
@@ -402,86 +419,104 @@
             wide += jnp.dot(wq_t[:, kk * per : (kk + 1) * per], hi, preferred_element_type=jnp.float32)
             thin += jnp.dot(wq_t[0:128, kk * per : (kk + 1) * per], lo, preferred_element_type=jnp.float32)
         block = (wide[0:128] + wide[128:256] + thin) * scale
-        gk_tx[lax.rem(i, n_pb)] = jnp.transpose(block, (1, 0))
-
-        @pl.when(i < n_pb)
+        gk_tx[i] = jnp.transpose(block, (1, 0))
+
+        @pl.when(i > 0)
         def _():
             gk_copy(i).start()
 
         return carry
 
+    many = n_pb // 2
+    for c in range(2):
+        diff_half(c)
+        lax.fori_loop(c * many, (c + 1) * many, key_block, 0)
+
     core, far = lax.rem(k, 2), k // 2
 
-    def query_rows(kk):
-        def block(n, total):
-            at = pl.ds(pl.multiple_of(n * 512, 512), 512)
-            key = ctx[at, :]
-            return total + (
-                jnp.dot(gated(kk, at, 512, d_hi), key, preferred_element_type=jnp.float32)
-                + jnp.dot(gated(kk, at, 512, d_lo), key, preferred_element_type=jnp.float32)
-            )
-
-        u_ref[kk] = lax.fori_loop(0, keys // 512, block, jnp.zeros((per, 128), jnp.float32))
-
-    def u_copy(x):
+    def query_rows(part, kk):
+        mask = jnp.concatenate(
+            [m_ref[kk, src * 64 + part * 32 : src * 64 + part * 32 + 32, :] for src in range(n_ha)], axis=0
+        ).reshape(n_ha, 32, keys)
+        hi = (mask * d_hi[kk, part * 32 : part * 32 + 32, :][None]).reshape(n_ha * 32, keys)
+        lo = (mask * d_lo[kk, part * 32 : part * 32 + 32, :][None]).reshape(n_ha * 32, keys)
+        key = ctx[...]
+        u_ref[part, kk] = jnp.dot(hi, key, preferred_element_type=jnp.float32) + jnp.dot(
+            lo, key, preferred_element_type=jnp.float32
+        )
+
+    def u_copy(part, x):
         return copy_to(
-            u_ref.at[x * 2 + 1 - core], u_rx.at[x], u_s.at[x], u_r.at[x], {"ka": far * 2 + 1 - core}
-        )
-
-    v_copy = copy_to(v_ref.at[1 - far], v_rx, v_s.at[0], v_r.at[0], {"ka": (1 - far) * 2 + core})
-    early_blocks = n_pb // 2
-    lax.fori_loop(0, early_blocks, key_block, 0)
-    for x in range(2):
-        query_rows(x * 2 + 1 - core)
-        u_copy(x).start()
-    for first in range(2):
-        x = 1 - far if first == 0 else far
-        query_rows(x * 2 + core)
-        u_copy(x).wait_recv()
-        v_ref[x] = u_ref[x * 2 + core] + u_rx[x]
-        if first == 0:
-            v_copy.start()
-    lax.fori_loop(early_blocks, n_pb, key_block, 0)
-
-    v_copy.wait_recv()
-    r_ref[...] = (v_ref[far] + v_rx[...]) * scale
-
-    def o_copy(i):
+            u_ref.at[part, x * 2 + 1 - core], u_rx.at[part, x], u_s.at[part, x], u_r.at[part, x],
+            {"ka": far * 2 + 1 - core},
+        )
+
+    def v_copy(part):
+        return copy_to(
+            v_ref.at[part, 1 - far], v_rx.at[part], v_s.at[part], v_r.at[part], {"ka": (1 - far) * 2 + core}
+        )
+
+    def o_copy(part, i):
         dest = lax.rem(h + i, n_ha)
         return copy_to(
-            r_ref.at[pl.ds(pl.multiple_of(dest * 64, 64), 64), :], o_rx.at[h], o_s.at[i], o_r.at[i], ha_dev(i)
-        )
-
-    for i in range(1, n_ha):
-        o_copy(i).start()
+            r_ref.at[part, pl.ds(pl.multiple_of(dest * 32, 32), 32), :],
+            o_rx.at[h, part * 32 : part * 32 + 32, :],
+            o_s.at[part, i], o_r.at[part, i], ha_dev(i),
+        )
+
+    def z_copy(i):
+        return copy_to(z_tx.at[lax.rem(h + i, n_ha)], z_rx.at[i], z_s.at[i], z_r.at[i], ha_dev(i))
+
+    def y_copy(i):
+        return copy_to(zsum.at[h], zsum.at[h], y_s.at[i], y_r.at[i], ha_dev(i))
+
+    def other_core(part):
+        for x in range(2):
+            query_rows(part, x * 2 + 1 - core)
+            u_copy(part, x).start()
+
+    def own_core(part):
+        for first in range(2):
+            x = 1 - far if first == 0 else far
+            query_rows(part, x * 2 + core)
+            u_copy(part, x).wait_recv()
+            v_ref[part, x] = u_ref[part, x * 2 + core] + u_rx[part, x]
+            if first == 0:
+                v_copy(part).start()
+
+    def to_owners(part):
+        v_copy(part).wait_recv()
+        r_ref[part] = (v_ref[part, far] + v_rx[part]) * scale
+        for i in range(1, n_ha):
+            o_copy(part, i).start()
+        o_rx[h, part * 32 : part * 32 + 32, :] = r_ref[part, pl.ds(pl.multiple_of(h * 32, 32), 32), :]
+
+    other_core(0)
+    own_core(0)
+    other_core(1)
+    to_owners(0)
 
     own = gk_tx[0]
     for i in range(1, n_pb):
         gk_copy(i).wait_recv()
         own = own + gk_rx[i]
     z_tx[...] = own.reshape(n_ha, 256 // n_ha, 128)
-
-    def z_copy(i):
-        return copy_to(z_tx.at[lax.rem(h + i, n_ha)], z_rx.at[i], z_s.at[i], z_r.at[i], ha_dev(i))
-
     for i in range(1, n_ha):
         z_copy(i).start()
 
+    own_core(1)
     mine = z_tx[h]
     for i in range(1, n_ha):
         z_copy(i).wait_recv()
         mine = mine + z_rx[i]
     zsum[h] = mine
-
-    def y_copy(i):
-        return copy_to(zsum.at[h], zsum.at[h], y_s.at[i], y_r.at[i], ha_dev(i))
-
     for i in range(1, n_ha):
         y_copy(i).start()
-
-    o_rx[h] = r_ref[pl.ds(pl.multiple_of(h * 64, 64), 64), :]
-    for i in range(1, n_ha):
-        o_copy(i).wait_recv()
+    to_owners(1)
+
+    for part in range(2):
+        for i in range(1, n_ha):
+            o_copy(part, i).wait_recv()
     for b in range(4):
         at = slice(b * LANES, (b + 1) * LANES)
         u = o_rx[2 * b : 2 * b + 2].reshape(LANES, 128)
@@ -500,10 +535,11 @@
         iq_copy(i).wait_send()
         wc_copy(i).wait_send()
         z_copy(i).wait_send()
-        o_copy(i).wait_send()
+        for part in range(2):
+            o_copy(part, i).wait_send()
         y_copy(i).wait_send()
     for i in range(1, n_ka):
-        for st in range(2):
+        for st in range(len(spans)):
             st_copy(st, i).wait_send()
         ix_copy(i).wait_send()
     for a in range(half):
@@ -512,9 +548,10 @@
                 ra_copy(a, c).wait_send()
             if a or c == 1:
                 rb_copy(a, c).wait_send()
-    for x in range(2):
-        u_copy(x).wait_send()
-    v_copy.wait_send()
+    for part in range(2):
+        for x in range(2):
+            u_copy(part, x).wait_send()
+        v_copy(part).wait_send()
 
 
 def body(sizes, main_query, main_key, index_query, index_weight, index_key, query_pos):
@@ -533,7 +570,8 @@
     wc = jnp.concatenate([wc, pos], axis=1)
 
     half = n_ha // 2
-    rows = half * 32
+    firsts, rows = stages(n_ha)
+    n_st = len(firsts) - 1
     per = n_ha * 64
     f32, bf16 = jnp.float32, jnp.bfloat16
     scratch = [
@@ -545,12 +583,12 @@
         pltpu.VMEM((rows, keys), f32),
         pltpu.VMEM((rows, keys), f32),
         pltpu.VMEM((heads + EXTRA, rows, keys), f32),
-        pltpu.VMEM((2, heads, rows, LANES), f32),
-        pltpu.VMEM((rows, LANES), f32),
-        pltpu.VMEM((rows, LANES), f32),
-        pltpu.VMEM((2, 2 * heads, rows), f32),
-        pltpu.VMEM((2, n_ka, 2 * heads, rows), f32),
-        pltpu.VMEM((LANES, rows), f32),
+        pltpu.VMEM((heads, t, LANES), f32),
+        pltpu.VMEM((t, LANES), f32),
+        pltpu.VMEM((t, LANES), f32),
+        pltpu.VMEM((n_st, 2 * heads, t), f32),
+        pltpu.VMEM((n_st, n_ka, 2 * heads, t), f32),
+        pltpu.VMEM((LANES, t), f32),
         pltpu.VMEM((n_ha, 2, 32, keys // 2), f32),
         pltpu.VMEM((half, 2, 32, keys // 2), f32),
         pltpu.VMEM((half, 2, 32, keys // 2), f32),
@@ -566,11 +604,11 @@
         pltpu.VMEM((n_ka, 64, keys), bf16),
         pltpu.VMEM((2, 32, LANES), f32),
         pltpu.VMEM((n_ka, 2, 32, LANES), f32),
-        pltpu.VMEM((n_ka, per, 128), f32),
-        pltpu.VMEM((2, per, 128), f32),
-        pltpu.VMEM((2, per, 128), f32),
-        pltpu.VMEM((per, 128), f32),
-        pltpu.VMEM((per, 128), f32),
+        pltpu.VMEM((2, n_ka, per // 2, 128), f32),
+        pltpu.VMEM((2, 2, per // 2, 128), f32),
+        pltpu.VMEM((2, 2, per // 2, 128), f32),
+        pltpu.VMEM((2, per // 2, 128), f32),
+        pltpu.VMEM((2, per // 2, 128), f32),
         pltpu.VMEM((n_ha, 64, 128), f32),
         pltpu.VMEM((n_pb, 256, 128), f32),
         pltpu.VMEM((n_pb, 256, 128), f32),
@@ -581,8 +619,8 @@
     dma = pltpu.SemaphoreType.DMA
     sems = [dma((NBUF,))]
     for shape in (
-        (2, n_ka), (half, 2), (half, 2), (n_ha,), (n_ha,), (n_pb,),
-        (n_ka,), (2,), (1,), (n_ha,), (n_pb,), (n_ha,), (n_ha,),
+        (n_st, n_ka), (half, 2), (half, 2), (n_ha,), (n_ha,), (n_pb,),
+        (n_ka,), (2, 2), (2,), (2, n_ha), (n_pb,), (n_ha,), (n_ha,),
     ):
         sems += [dma(shape), dma(shape)]
     vmem = pl.BlockSpec(memory_space=pltpu.VMEM)

time: 101 us -> 96.5 us (0.955); the launches traced: 101 us -> 95.2 us
  Pallas kernels: 93.2 us -> 87.4 us
    pallas_call x1, Pallas kernels: 93.2 us -> 87.4 us  [body(): pl.pallas_call(functools.partial(kernel, dims), out_shape=(jax.ShapeDtype...]
where the time goes in v3:
time: 96.5 us; the launch traced here: 95.2 us
  Pallas kernels  87.4 us (91%)
  local copies, waits for them, and re-layouts  5.88 us (6%)
  other arithmetic  1.31 us (1%)
    pallas_call x1, Pallas kernels, body(): pl.pallas_call(functools.partial(kernel, dims), out_shape=(jax.ShapeDtype...  87.4 us
    unnamed x3, local copies, waits for them, and re-layouts  3.9 us

profile of v3, /device:TPU:8, one launch (start us, length us, event | category | flops | bytes accessed | tf_op | source)
XLA Modules:
  0.0 95.2 jit_solution(15665777187405406484)
XLA Ops:
  0.6 0.7 convert_element_type.6
  1.3 0.1 reshape.32
  1.4 0.1 reshape.33
  1.5 0.8 copy.10
  2.3 0.1 reshape.39
  2.4 0.1 reshape.36
  2.5 0.6 select_maximum_fusion.wc_ref
  3.1 87.4 %shard_map.85 = (f32[512,128]{1,0:T(8,128)}, f32[8,512]{1,0:T(8,128)}, f32[256,128]{1,0:T(8,128)}) custom-call(bf16[16,192,256]{2,1,0:T(8,128)(2,1)} %bitcast.7, bf16[16,192,2048]{2,1,0:T(8,128)(2,1)} %bitcast.6, bf16[4,512,128]{2,1,0:T(8,128)(2,1)} %bitcast.8, f32[8,8,128]{2,1,0:T(8,128)} %select_maximum_fusion.wc_ref, bf16[256,128]{1,0:T(8,128)(2,1)} %ik_ref.1), custom_call_target="tpu_custom_call" | custom-call | tf_op jit(solution)/shard_map/pallas_call | solution.py:627
  90.5 0.7 slice_reduce_fusion
  91.3 0.1 reshape_squeeze.3
  91.3 0.7 copy.13
  92.0 1.7 %copy.16 = f32[64,8,128]{2,1,0:T(8,128)} copy(f32[64,8,128]{2,1,0:T(8,128)} %bitcast.9) | data formatting | bytes 524288
  93.7 1.6 %copy.17 = f32[256,128]{1,0:T(8,128)} copy(f32[256,128]{1,0:T(8,128)} %get-tuple-element.20) | data formatting | bytes 262144
  (2 shorter events, 0.0 us)

commit v4 on v3

--- a/solution.py
+++ b/solution.py
@@ -349,12 +349,7 @@
     for c in (1, 0):
         chain_a(2, c)
         chain_b(2, 1 - c)
-    lax.fori_loop(0, total_parts // 4, index_part, 0)
-    finish(2)
-    lax.fori_loop(total_parts // 4, total_parts, index_part, 0)
-    for c in range(2):
-        chain_a(3, c)
-        chain_b(3, c)
+    lax.fori_loop(0, total_parts, index_part, 0)
 
     rel = pos_ref[n_ha - 1][:, 0:1] - first_key
     seen = lax.broadcasted_iota(jnp.int32, (32, keys), 1) <= rel
@@ -371,6 +366,10 @@
 
     for i in range(1, n_ka):
         ix_copy(i).start()
+    finish(2)
+    for c in range(2):
+        chain_a(3, c)
+        chain_b(3, c)
     for i in range(1, n_ka):
         ix_copy(i).wait_recv()
     tops = [ix_tx[0]] + [ix_rx[i, 0] for i in range(1, n_ka)]
@@ -470,19 +469,14 @@
     def y_copy(i):
         return copy_to(zsum.at[h], zsum.at[h], y_s.at[i], y_r.at[i], ha_dev(i))
 
-    def other_core(part):
-        for x in range(2):
-            query_rows(part, x * 2 + 1 - core)
-            u_copy(part, x).start()
-
-    def own_core(part):
-        for first in range(2):
-            x = 1 - far if first == 0 else far
-            query_rows(part, x * 2 + core)
-            u_copy(part, x).wait_recv()
-            v_ref[part, x] = u_ref[part, x * 2 + core] + u_rx[part, x]
-            if first == 0:
-                v_copy(part).start()
+    def other_core(part, x):
+        query_rows(part, x * 2 + 1 - core)
+        u_copy(part, x).start()
+
+    def own_core(part, x):
+        query_rows(part, x * 2 + core)
+        u_copy(part, x).wait_recv()
+        v_ref[part, x] = u_ref[part, x * 2 + core] + u_rx[part, x]
 
     def to_owners(part):
         v_copy(part).wait_recv()
@@ -491,10 +485,14 @@
             o_copy(part, i).start()
         o_rx[h, part * 32 : part * 32 + 32, :] = r_ref[part, pl.ds(pl.multiple_of(h * 32, 32), 32), :]
 
-    other_core(0)
-    own_core(0)
-    other_core(1)
-    to_owners(0)
+    for part in range(2):
+        other_core(part, 1 - far)
+        own_core(part, 1 - far)
+        v_copy(part).start()
+    for part in range(2):
+        other_core(part, far)
+        own_core(part, far)
+        to_owners(part)
 
     own = gk_tx[0]
     for i in range(1, n_pb):
@@ -503,8 +501,6 @@
     z_tx[...] = own.reshape(n_ha, 256 // n_ha, 128)
     for i in range(1, n_ha):
         z_copy(i).start()
-
-    own_core(1)
     mine = z_tx[h]
     for i in range(1, n_ha):
         z_copy(i).wait_recv()
@@ -512,17 +508,24 @@
     zsum[h] = mine
     for i in range(1, n_ha):
         y_copy(i).start()
-    to_owners(1)
 
     for part in range(2):
         for i in range(1, n_ha):
             o_copy(part, i).wait_recv()
+    weight_sums = jnp.zeros((8, 64), jnp.float32)
     for b in range(4):
         at = slice(b * LANES, (b + 1) * LANES)
         u = o_rx[2 * b : 2 * b + 2].reshape(LANES, 128)
         gq_ref[at, :] = u * w_own[at, :]
         dots = jnp.transpose(u * iq_ref[k, at, :].astype(jnp.float32), (1, 0))
-        gw_ref[:, at] = jnp.broadcast_to(jnp.sum(dots, axis=0, keepdims=True), (8, LANES))
+        sums = jnp.broadcast_to(jnp.sum(dots, axis=0, keepdims=True), (8, LANES))
+        sums = jnp.where(lax.rem(lane, 8) == lax.broadcasted_iota(jnp.int32, (8, LANES), 0), sums, 0.0)
+        row = lax.broadcasted_iota(jnp.int32, (LANES, 64), 0) // 8 + b * (LANES // 8)
+        pick = jnp.where(row == lax.broadcasted_iota(jnp.int32, (LANES, 64), 1), 1.0, 0.0)
+        weight_sums = weight_sums + jnp.dot(
+            sums, pick, precision=lax.Precision.HIGHEST, preferred_element_type=jnp.float32
+        )
+    gw_ref[...] = weight_sums
 
     for i in range(1, n_ha):
         y_copy(i).wait_recv()
@@ -552,6 +555,15 @@
         for x in range(2):
             u_copy(part, x).wait_send()
         v_copy(part).wait_send()
+
+
+def hand_over(gq_in, gw_in, gk_in, gq_out, gw_out, gk_out, sems):
+    pairs = ((gq_in, gq_out), (gw_in, gw_out), (gk_in, gk_out))
+    copies = [pltpu.make_async_copy(a, b, sems.at[n]) for n, (a, b) in enumerate(pairs)]
+    for copy in copies:
+        copy.start()
+    for copy in copies:
+        copy.wait()
 
 
 def body(sizes, main_query, main_key, index_query, index_weight, index_key, query_pos):
@@ -628,7 +640,7 @@
         functools.partial(kernel, dims),
         out_shape=(
             jax.ShapeDtypeStruct((per, 128), f32),
-            jax.ShapeDtypeStruct((8, per), f32),
+            jax.ShapeDtypeStruct((8, 64), f32),
             jax.ShapeDtypeStruct((256, 128), f32),
         ),
         in_specs=[vmem, pl.BlockSpec(memory_space=pl.ANY)] + [vmem] * 3,
@@ -638,7 +650,15 @@
             collective_id=0, has_side_effects=True, vmem_limit_bytes=63 * 1024 * 1024
         ),
     )(qt, kt, iq, wc, index_key)
-    return (gq.reshape(t // n_ka, joined, 128), gw[0].reshape(t // n_ka, joined), gk)
+    hbm = pl.BlockSpec(memory_space=pl.ANY)
+    gq, gw, gk = pl.pallas_call(
+        hand_over,
+        out_shape=tuple(jax.ShapeDtypeStruct(x.shape, f32) for x in (gq, gw, gk)),
+        in_specs=[hbm] * 3,
+        out_specs=(hbm,) * 3,
+        scratch_shapes=[dma((3,))],
+    )(gq, gw, gk)
+    return (gq.reshape(t // n_ka, joined, 128), gw.T, gk)
 
 
 def solution(mesh):

time: 96.5 us -> 106 us (1.098)
  Pallas kernels: 87.4 us -> 102 us
  local copies, waits for them, and re-layouts: 5.88 us -> 1.16 us
    pallas_call x0 -> x1, Pallas kernels: none -> 13.2 us  [body(): pl.pallas_call(hand_over, out_shape=tuple((jax.ShapeDtypeStruct(x.shape,...]
    unnamed x3 -> x0, local copies, waits for them, and re-layouts: 3.9 us -> none
    pallas_call x1, Pallas kernels: 87.4 us -> 89.2 us  [body(): pl.pallas_call(functools.partial(kernel, dims), out_shape=(jax.ShapeDtype...]
where the time goes in v4:
time: 106 us
  Pallas kernels  102 us (96%)
  other arithmetic  1.31 us (1%)
  local copies, waits for them, and re-layouts  1.16 us (1%)
    pallas_call x1, Pallas kernels, body(): pl.pallas_call(functools.partial(kernel, dims), out_shape=(jax.ShapeDtype...  89.2 us
    pallas_call x1, Pallas kernels, body(): pl.pallas_call(hand_over, out_shape=tuple((jax.ShapeDtypeStruct(x.shape,...  13.2 us

profile of v4, /device:TPU:8, one launch (start us, length us, event | category | flops | bytes accessed | tf_op | source)
XLA Modules:
  0.0 105.6 jit_solution(2436336921965275044)
XLA Ops:
  0.6 0.7 convert_element_type.6
  1.3 0.1 reshape.32
  1.4 0.1 reshape.33
  1.5 0.8 copy.9
  2.3 0.1 reshape.39
  2.4 0.1 reshape.36
  2.5 0.6 select_maximum_fusion.wc_ref
  3.1 89.2 %shard_map.85 = (f32[512,128]{1,0:T(8,128)}, f32[8,64]{1,0:T(8,128)}, f32[256,128]{1,0:T(8,128)}) custom-call(bf16[16,192,256]{2,1,0:T(8,128)(2,1)} %bitcast.8, bf16[16,192,2048]{2,1,0:T(8,128)(2,1)} %bitcast.7, bf16[4,512,128]{2,1,0:T(8,128)(2,1)} %bitcast.9, f32[8,8,128]{2,1,0:T(8,128)} %select_maximum_fusion.wc_ref, bf16[256,128]{1,0:T(8,128)(2,1)} %ik_ref.1), custom_call_target="tpu_custom_call" | custom-call | tf_op jit(solution)/shard_map/pallas_call | solution.py:639
  92.3 13.2 %shard_map.86 = (f32[512,128]{1,0:T(8,128)}, f32[8,64]{1,0:T(8,128)}, f32[256,128]{1,0:T(8,128)}) custom-call(f32[512,128]{1,0:T(8,128)} %get-tuple-element.9.gq_in, f32[8,64]{1,0:T(8,128)} %get-tuple-element.10.gw_in, f32[256,128]{1,0:T(8,128)} %get-tuple-element.11.gk_in), custom_call_target="tpu_custom_call" | custom-call | tf_op jit(solution)/shard_map/pallas_call | solution.py:654
  (2 shorter events, 0.0 us)

commit v5 on v4

--- a/solution.py
+++ b/solution.py
@@ -407,8 +407,8 @@
         return (m_ref[kk, :, at].reshape(n_ha, 64, width) * d_ref[kk, :, at][None]).reshape(per, width)
 
     def key_block(n, carry):
-        dest = (n // many) * many + lax.rem(p + n, many)
-        i = lax.rem(dest - p + n_pb, n_pb)
+        i = lax.rem(n + 1, n_pb)
+        dest = lax.rem(p + n + 1, n_pb)
         at = pl.ds(pl.multiple_of(dest * 256, 256), 256)
         wide = jnp.zeros((256, 256), jnp.float32)
         thin = jnp.zeros((128, 256), jnp.float32)
@@ -426,10 +426,9 @@
 
         return carry
 
-    many = n_pb // 2
     for c in range(2):
         diff_half(c)
-        lax.fori_loop(c * many, (c + 1) * many, key_block, 0)
+    lax.fori_loop(0, n_pb, key_block, 0)
 
     core, far = lax.rem(k, 2), k // 2
 
@@ -492,7 +491,8 @@
     for part in range(2):
         other_core(part, far)
         own_core(part, far)
-        to_owners(part)
+        if part == 0:
+            to_owners(0)
 
     own = gk_tx[0]
     for i in range(1, n_pb):
@@ -501,6 +501,7 @@
     z_tx[...] = own.reshape(n_ha, 256 // n_ha, 128)
     for i in range(1, n_ha):
         z_copy(i).start()
+    to_owners(1)
     mine = z_tx[h]
     for i in range(1, n_ha):
         z_copy(i).wait_recv()
@@ -555,15 +556,6 @@
         for x in range(2):
             u_copy(part, x).wait_send()
         v_copy(part).wait_send()
-
-
-def hand_over(gq_in, gw_in, gk_in, gq_out, gw_out, gk_out, sems):
-    pairs = ((gq_in, gq_out), (gw_in, gw_out), (gk_in, gk_out))
-    copies = [pltpu.make_async_copy(a, b, sems.at[n]) for n, (a, b) in enumerate(pairs)]
-    for copy in copies:
-        copy.start()
-    for copy in copies:
-        copy.wait()
 
 
 def body(sizes, main_query, main_key, index_query, index_weight, index_key, query_pos):
@@ -650,14 +642,6 @@
             collective_id=0, has_side_effects=True, vmem_limit_bytes=63 * 1024 * 1024
         ),
     )(qt, kt, iq, wc, index_key)
-    hbm = pl.BlockSpec(memory_space=pl.ANY)
-    gq, gw, gk = pl.pallas_call(
-        hand_over,
-        out_shape=tuple(jax.ShapeDtypeStruct(x.shape, f32) for x in (gq, gw, gk)),
-        in_specs=[hbm] * 3,
-        out_specs=(hbm,) * 3,
-        scratch_shapes=[dma((3,))],
-    )(gq, gw, gk)
     return (gq.reshape(t // n_ka, joined, 128), gw.T, gk)
 
 

time: 106 us -> 97.4 us (0.919); the launches traced: 106 us -> 95.7 us
  Pallas kernels: 102 us -> 88.1 us
  local copies, waits for them, and re-layouts: 1.16 us -> 5.66 us
    pallas_call x1 -> x0, Pallas kernels: 13.2 us -> none  [body(): pl.pallas_call(hand_over, out_shape=tuple((jax.ShapeDtypeStruct(x.shape,...]
    unnamed x0 -> x3, local copies, waits for them, and re-layouts: none -> 4.5 us
    pallas_call x1, Pallas kernels: 89.2 us -> 88.1 us  [body(): pl.pallas_call(functools.partial(kernel, dims), out_shape=(jax.ShapeDtype...]
where the time goes in v5:
time: 97.4 us; the launch traced here: 95.7 us
  Pallas kernels  88.1 us (90%)
  local copies, waits for them, and re-layouts  5.66 us (6%)
  other arithmetic  1.31 us (1%)
    pallas_call x1, Pallas kernels, body(): pl.pallas_call(functools.partial(kernel, dims), out_shape=(jax.ShapeDtype...  88.1 us
    unnamed x3, local copies, waits for them, and re-layouts  4.5 us

profile of v5, /device:TPU:8, one launch (start us, length us, event | category | flops | bytes accessed | tf_op | source)
XLA Modules:
  0.0 95.7 jit_solution(7312239161716521956)
XLA Ops:
  0.6 0.7 convert_element_type.6
  1.3 0.1 reshape.32
  1.4 0.1 reshape.33
  1.5 0.8 copy.9
  2.3 0.1 reshape.39
  2.4 0.1 reshape.36
  2.5 0.6 select_maximum_fusion.wc_ref
  3.1 88.1 %shard_map.85 = (f32[512,128]{1,0:T(8,128)}, f32[8,64]{1,0:T(8,128)}, f32[256,128]{1,0:T(8,128)}) custom-call(bf16[16,192,256]{2,1,0:T(8,128)(2,1)} %bitcast.8, bf16[16,192,2048]{2,1,0:T(8,128)(2,1)} %bitcast.7, bf16[4,512,128]{2,1,0:T(8,128)(2,1)} %bitcast.9, f32[8,8,128]{2,1,0:T(8,128)} %select_maximum_fusion.wc_ref, bf16[256,128]{1,0:T(8,128)(2,1)} %ik_ref.1), custom_call_target="tpu_custom_call" | custom-call | tf_op jit(solution)/shard_map/pallas_call | solution.py:631
  91.2 1.7 %copy.15 = f32[64,8,128]{2,1,0:T(8,128)} copy(f32[64,8,128]{2,1,0:T(8,128)} %bitcast.10) | data formatting | bytes 524288
  92.9 1.3 %copy.16 = f32[64,8]{0,1:T(8,128)} copy(f32[64,8]{0,1:T(8,128)} %bitcast.13) | data formatting | bytes 4096
  94.2 1.6 %copy.17 = f32[256,128]{1,0:T(8,128)} copy(f32[256,128]{1,0:T(8,128)} %get-tuple-element.14) | data formatting | bytes 262144
  (2 shorter events, 0.0 us)

commit v6 on v3

--- a/solution.py
+++ b/solution.py
@@ -517,12 +517,20 @@
     for part in range(2):
         for i in range(1, n_ha):
             o_copy(part, i).wait_recv()
+    weight_sums = jnp.zeros((8, 64), jnp.float32)
     for b in range(4):
         at = slice(b * LANES, (b + 1) * LANES)
         u = o_rx[2 * b : 2 * b + 2].reshape(LANES, 128)
         gq_ref[at, :] = u * w_own[at, :]
         dots = jnp.transpose(u * iq_ref[k, at, :].astype(jnp.float32), (1, 0))
-        gw_ref[:, at] = jnp.broadcast_to(jnp.sum(dots, axis=0, keepdims=True), (8, LANES))
+        sums = jnp.broadcast_to(jnp.sum(dots, axis=0, keepdims=True), (8, LANES))
+        sums = jnp.where(lax.rem(lane, 8) == lax.broadcasted_iota(jnp.int32, (8, LANES), 0), sums, 0.0)
+        row = lax.broadcasted_iota(jnp.int32, (LANES, 64), 0) // 8 + b * (LANES // 8)
+        pick = jnp.where(row == lax.broadcasted_iota(jnp.int32, (LANES, 64), 1), 1.0, 0.0)
+        weight_sums = weight_sums + jnp.dot(
+            sums, pick, precision=lax.Precision.HIGHEST, preferred_element_type=jnp.float32
+        )
+    gw_ref[...] = weight_sums
 
     for i in range(1, n_ha):
         y_copy(i).wait_recv()
@@ -552,6 +560,12 @@
         for x in range(2):
             u_copy(part, x).wait_send()
         v_copy(part).wait_send()
+
+
+def hand_over(gq_in, gw_in, gk_in, gq_out, gw_out, gk_out):
+    gq_out[...] = gq_in[...]
+    gw_out[...] = gw_in[...]
+    gk_out[...] = gk_in[...]
 
 
 def body(sizes, main_query, main_key, index_query, index_weight, index_key, query_pos):
@@ -628,7 +642,7 @@
         functools.partial(kernel, dims),
         out_shape=(
             jax.ShapeDtypeStruct((per, 128), f32),
-            jax.ShapeDtypeStruct((8, per), f32),
+            jax.ShapeDtypeStruct((8, 64), f32),
             jax.ShapeDtypeStruct((256, 128), f32),
         ),
         in_specs=[vmem, pl.BlockSpec(memory_space=pl.ANY)] + [vmem] * 3,
@@ -638,7 +652,13 @@
             collective_id=0, has_side_effects=True, vmem_limit_bytes=63 * 1024 * 1024
         ),
     )(qt, kt, iq, wc, index_key)
-    return (gq.reshape(t // n_ka, joined, 128), gw[0].reshape(t // n_ka, joined), gk)
+    gq, gw, gk = pl.pallas_call(
+        hand_over,
+        out_shape=tuple(jax.ShapeDtypeStruct(x.shape, f32) for x in (gq, gw, gk)),
+        in_specs=[vmem] * 3,
+        out_specs=(vmem,) * 3,
+    )(gq, gw, gk)
+    return (gq.reshape(t // n_ka, joined, 128), gw.T, gk)
 
 
 def solution(mesh):

time: 96.5 us -> 93.6 us (0.970)
  local copies, waits for them, and re-layouts: 5.88 us -> 1.16 us
  Pallas kernels: 87.4 us -> 89.6 us
    unnamed x3 -> x0, local copies, waits for them, and re-layouts: 3.9 us -> none
    pallas_call x0 -> x1, Pallas kernels: none -> 1.75 us  [body(): pl.pallas_call(hand_over, out_shape=tuple((jax.ShapeDtypeStruct(x.shape,...]
where the time goes in v6:
time: 93.6 us; the launch traced here: 92.8 us
  Pallas kernels  89.6 us (96%)
  other arithmetic  1.31 us (1%)
  local copies, waits for them, and re-layouts  1.16 us (1%)
    pallas_call x1, Pallas kernels, body(): pl.pallas_call(functools.partial(kernel, dims), out_shape=(jax.ShapeDtype...  87.9 us

profile of v6, /device:TPU:8, one launch (start us, length us, event | category | flops | bytes accessed | tf_op | source)
XLA Modules:
  0.0 92.8 jit_solution(12753546486628335153)
XLA Ops:
  0.6 0.7 convert_element_type.6
  1.3 0.1 reshape.32
  1.4 0.1 reshape.33
  1.5 0.8 copy.9
  2.3 0.1 reshape.39
  2.4 0.1 reshape.36
  2.5 0.6 select_maximum_fusion.wc_ref
  3.1 87.9 %shard_map.85 = (f32[512,128]{1,0:T(8,128)}, f32[8,64]{1,0:T(8,128)}, f32[256,128]{1,0:T(8,128)}) custom-call(bf16[16,192,256]{2,1,0:T(8,128)(2,1)} %bitcast.8, bf16[16,192,2048]{2,1,0:T(8,128)(2,1)} %bitcast.7, bf16[4,512,128]{2,1,0:T(8,128)(2,1)} %bitcast.9, f32[8,8,128]{2,1,0:T(8,128)} %select_maximum_fusion.wc_ref, bf16[256,128]{1,0:T(8,128)(2,1)} %ik_ref.1), custom_call_target="tpu_custom_call" | custom-call | tf_op jit(solution)/shard_map/pallas_call | solution.py:641
  91.0 1.7 %shard_map.86 = (f32[512,128]{1,0:T(8,128)}, f32[8,64]{1,0:T(8,128)}, f32[256,128]{1,0:T(8,128)}) custom-call(f32[512,128]{1,0:T(8,128)} %get-tuple-element.9.gq_in, f32[8,64]{1,0:T(8,128)} %get-tuple-element.10.gw_in, f32[256,128]{1,0:T(8,128)} %get-tuple-element.11.gk_in), custom_call_target="tpu_custom_call" | custom-call | tf_op jit(solution)/shard_map/pallas_call | solution.py:655
  (2 shorter events, 0.0 us)
